TPU v7x, 32 devices: a whole 2x2x4 slice. The times are simulated.
32 devices in a mesh: shard: 4 (over y, x), seq: 8 (over z, core).
Axes of the slice: x: 2, y: 2, z: 4, core: 2. Of those that a mesh axis runs over, the one named last changes fastest.
Arguments:
- queries: bfloat16 [64, 4096], P(('shard', 'seq')), may hold values from -25 to 25
- cached_keys: bfloat16 [8, 8192, 1024], P('shard', 'seq'), may hold values from -6 to 6
- cached_values: bfloat16 [8, 8192, 1024], P('shard', 'seq'), may hold values from -96 to 96
- shard_hits: int32 [64, 8], P(('shard', 'seq')), may hold values from 0 to 1, as said below
Outputs:
- attended: bfloat16 [64, 4096], P(('shard', 'seq'))
Inputs may be any that keep to these rules, and one draw needn't show every extreme that they name: `shard_hits`: each query lists 1 to 4 of the 8 shards. At most 32 queries list any one shard, and some shard is listed by exactly 32.
All inputs are finite; a program needn't handle non-finite values.
Results may differ from a plain program's by a relative error of at most 0.0035.
Values may be sent and summed in bfloat16 or wider, within the bound.
No kernel may reach another device: no remote copies, remote signals or barrier semaphores. Data moves between devices by JAX's collectives and lax.ppermute only.
A program may use at most 128 MiB of HBM per device.

v0:
```python
import math

import jax
import jax.numpy as jnp
from jax import lax
from jax.sharding import PartitionSpec as P

HD = 128
KB = 512


NEG_FILL = -1e30


def combine_states(earlier, later):
    max_a, den_a, num_a = earlier
    max_b, den_b, num_b = later
    maximum = jnp.maximum(max_a, max_b)
    factor_a = jnp.exp(max_a - maximum)
    factor_b = jnp.exp(max_b - maximum)
    return (
        maximum,
        den_a * factor_a + den_b * factor_b,
        num_a * factor_a[..., None] + num_b * factor_b[..., None],
    )


def empty_state(count_rows, kv_heads, group_size):
    return (
        jnp.full((count_rows, kv_heads, group_size), NEG_FILL, jnp.float32),
        jnp.zeros((count_rows, kv_heads, group_size), jnp.float32),
        jnp.zeros((count_rows, kv_heads, group_size, HD), jnp.float32),
    )


def block_scan(query_rows, listed, key_blocks, value_blocks, state):
    scale_factor = 1.0 / math.sqrt(HD)
    is_listed = (listed > 0)[:, None, None]

    def advance(running, block_pair):
        key_block, value_block = block_pair
        scores = (
            jnp.einsum("ngrd,tgd->ngrt", query_rows, key_block, preferred_element_type=jnp.float32)
            * scale_factor
        )
        block_peak = jnp.max(scores, axis=-1)
        weights = jnp.exp(scores - block_peak[..., None]).astype(jnp.bfloat16)
        block_total = jnp.sum(weights, axis=-1, dtype=jnp.float32)
        block_value = jnp.einsum(
            "ngrt,tgd->ngrd", weights, value_block, preferred_element_type=jnp.float32
        )
        block_peak = jnp.where(is_listed, block_peak, NEG_FILL)
        block_total = jnp.where(is_listed, block_total, 0.0)
        block_value = jnp.where(is_listed[..., None], block_value, 0.0)
        return (combine_states(running, (block_peak, block_total, block_value)), None)

    state, _ = lax.scan(advance, state, (key_blocks, value_blocks))
    return state


def shards(queries, cached_keys, cached_values, shard_hits):
    all_queries, all_hits = (
        lax.all_gather(queries, ("shard", "seq"), axis=0, tiled=True),
        lax.all_gather(shard_hits, ("shard", "seq"), axis=0, tiled=True),
    )
    count_rows = all_queries.shape[0]
    own_rows = queries.shape[0]
    local_shards = cached_keys.shape[0]
    kv_heads = cached_keys.shape[2] // HD
    group_size = all_queries.shape[1] // HD // kv_heads
    grouped = all_queries.reshape(count_rows, kv_heads, group_size, HD)
    local_hits = lax.dynamic_slice_in_dim(
        all_hits, lax.axis_index("shard") * local_shards, local_shards, 1
    )
    state = empty_state(count_rows, kv_heads, group_size)
    for shard_slot in range(local_shards):
        key_blocks = cached_keys[shard_slot].reshape(-1, KB, kv_heads, HD)
        value_blocks = cached_values[shard_slot].reshape(-1, KB, kv_heads, HD)
        listed = local_hits[:, shard_slot]
        state = block_scan(grouped, listed, key_blocks, value_blocks, state)
    maximum = state[0].reshape(count_rows, -1)
    denominator = state[1].reshape(count_rows, -1)
    numerator = state[2].reshape(count_rows, -1, HD)
    overall = lax.pmax(maximum.astype(jnp.bfloat16), ("shard", "seq")).astype(maximum.dtype)
    factor = jnp.exp(maximum - overall)
    numerators, denominators = (
        lax.psum_scatter(
            numerator * factor[..., None], ("shard", "seq"), scatter_dimension=0, tiled=True
        ),
        lax.psum_scatter(denominator * factor, ("shard", "seq"), scatter_dimension=0, tiled=True),
    )
    merged = numerators / denominators[..., None]
    return merged.reshape(own_rows, -1).astype(jnp.bfloat16)


def solution(mesh):
    in_specs = (
        P(("shard", "seq"), None),
        P("shard", "seq", None),
        P("shard", "seq", None),
        P(("shard", "seq"), None),
    )
    out_specs = P(("shard", "seq"), None)
    return jax.shard_map(shards, mesh=mesh, in_specs=in_specs, out_specs=out_specs, check_vma=False)
```

profile of v0, /device:TPU:0, one launch (start us, length us, event | category | flops | bytes accessed | tf_op | source)
XLA Modules:
  0.0 306.1 jit_solution(10584462241885124811)
XLA Ops:
  6.5 43.5 %all-gather = s32[32,2,8]{2,1,0:T(2,128)S(1)} all-gather(s32[1,2,8]{2,1,0:T(2,128)} %bitcast.149), channel_id=1, replica_groups=mesh['shard'=4,'seq'=8] {'shard','seq'}, dimensions={0}, use_global_device_ids=true | all-gather | bytes 2112 | tf_op jit(solution)/shard_map/all_gather | solution.py:64
  50.3 39.1 %all-gather.1 = bf16[32,2,4096]{2,1,0:T(2,128)(2,1)S(1)} all-gather(bf16[1,2,4096]{2,1,0:T(2,128)(2,1)} %bitcast.148), channel_id=1, replica_groups=mesh['shard'=4,'seq'=8] {'shard','seq'}, dimensions={0}, use_global_device_ids=true | all-gather | bytes 540672 | tf_op jit(solution)/shard_map/all_gather | solution.py:63
  90.1 3.2 %slice_bitcast_fusion.1 = (bf16[128,8,8,128]{3,1,2,0:T(8,128)(2,1)S(1)}, bf16[128,8,8,128]{3,1,2,0:T(8,128)(2,1)S(1)}) fusion(bf16[2,1024,1024]{2,1,0:T(8,128)(2,1)} %param.9), kind=kLoop, calls=%fused_computation.41 | loop fusion | bytes 8388608
  93.3 2.0 copy.44
  95.2 2.0 copy.42
  98.2 1.9 copy.45
  100.1 2.0 copy.43
  102.1 10.3 %while.30 = (s32[]{:T(128)}, f32[64,8,4]{0,2,1:T(4,128)S(1)}, f32[64,8,4]{0,2,1:T(4,128)S(1)}, f32[64,8,4,128]{3,0,2,1:T(8,128)S(1)}, pred[64,1,1]{0,2,1:T(4,128...) while((s32[]{:T(128)}, f32[64,8,4]{0,2,1:T(4,128)S(1)}, ...), condition=%wide.region_3.4_spmd.clone, body=%wide.region_0.3_spmd.clone.sunk | while | flops 548683776 | bytes 21610756 | solution.py:57
  102.1 1.7 constant_dynamic-slice_fusion.8
  104.5 1.2 convert_reduce_fusion.5
  105.8 1.3 fusion.34
  107.2 1.7 constant_dynamic-slice_fusion.8
  109.7 1.2 convert_reduce_fusion.5
  111.0 1.3 fusion.34
  112.3 10.1 %while.29 = (s32[]{:T(128)}, f32[64,8,4]{0,2,1:T(4,128)S(1)}, f32[64,8,4]{0,2,1:T(4,128)S(1)}, f32[64,8,4,128]{3,0,2,1:T(8,128)S(1)}, pred[64,1,1]{0,2,1:T(4,128...) while((s32[]{:T(128)}, f32[64,8,4]{0,2,1:T(4,128)S(1)}, ...), condition=%wide.region_7.8_spmd, body=%wide.region_4.7_spmd.sunk | while | flops 548417536 | bytes 21610736 | solution.py:57
  112.3 1.7 constant_dynamic-slice_fusion.7
  114.8 1.2 convert_reduce_fusion.4
  116.1 1.3 fusion.30
  117.4 1.7 constant_dynamic-slice_fusion.7
  121.2 1.3 fusion.30
  122.5 39.4 %pmax.7 = bf16[64,32]{0,1:T(8,128)(2,1)S(1)} all-reduce(bf16[64,32]{0,1:T(8,128)(2,1)S(1)} %convert_element_type.24), channel_id=1, replica_groups=mesh['shard'=4,'seq'=8] {'shard','seq'}, use_global_device_ids=true, to_apply=%region_8.9 | all-reduce | flops 2048 | bytes 8192 | tf_op jit(solution)/shard_map/pmax | solution.py:84
  162.0 1.7 copy_multiply_fusion
  163.7 39.2 %all-reduce = f32[64,32]{0,1:T(8,128)S(1)} all-reduce(f32[64,32]{0,1:T(8,128)S(1)} %get-tuple-element.219), channel_id=3, replica_groups=mesh['shard'=4,'seq'=8] {'shard','seq'}, use_global_device_ids=true, to_apply=%region_10.11.clone | all-reduce | flops 2048 | bytes 16384
  203.0 94.7 %reduce-scatter.3.cloned.1.call-done = f32[2,32,128]{2,1,0:T(8,128)} async-done(((f32[64,32,128]{2,1,0:T(8,128)}), f32[2,32,128]{2,1,0:T(8,128)}) %reduce-scatter.3.cloned.1.call-update) | async-done | bytes 32784 | tf_op jit(solution)/shard_map/reduce_scatter | solution.py:87
  (29 shorter events, 8.2 us)
Async XLA Ops:
  6.5 291.2 %reduce-scatter.3.cloned.1.call-start = ((), (), s32[]{:S(2)}) async-start(), calls=%async_computation.1 | async-start | bytes 1081344 | tf_op jit(solution)/shard_map/reduce_scatter | solution.py:87
  93.2 4.0 %copy-start = (bf16[2,1024,1024]{2,1,0:T(8,128)(2,1)S(1)}, bf16[2,1024,1024]{2,1,0:T(8,128)(2,1)}, u32[]{:S(2)}) copy-start(bf16[2,1024,1024]{2,1,0:T(8,128)(2,1)} %param.10) | copy-start | bytes 12582916
Sparse Core Ops, SparseCore 0:
  163.8 133.9 reduce-scatter.2
where the time goes:
time: 307 us; the launch traced here: 306 us
  blocking collectives  161 us (52%)
  waiting for transfers between devices  94.8 us (31%)
  local copies, waits for them, and re-layouts  20.3 us (7%)
  between operations  13.5 us (4%)
  matrix products  8.4 us (3%)
  other arithmetic  7.78 us (3%)
    reduce_scatter x1, waiting for transfers between devices, shards(): lax.psum_scatter(numerator * factor[..., None], ('shard', 'seq'), scatter...  94.7 us
    all_gather x1, blocking collectives, shards(): lax.all_gather(shard_hits, ('shard', 'seq'), axis=0, tiled=True)  43.5 us
    pmax x1, blocking collectives, shards(): lax.pmax(maximum.astype(jnp.bfloat16), ('shard', 'seq'))  39.4 us
    unnamed x1, blocking collectives  39.2 us
    all_gather x1, blocking collectives, shards(): lax.all_gather(queries, ('shard', 'seq'), axis=0, tiled=True)  39.1 us
    unnamed x13, local copies, waits for them, and re-layouts  13.1 us
    dynamic_slice x4, local copies, waits for them, and re-layouts, block_scan(): state, _ = lax.scan(advance, state, (key_blocks, value_blocks))  6.72 us
  transfers between devices with their start and end apart: 1, of which 1 were waited for; matrix products, arithmetic and copies ran while one was open for 0% of the time, Pallas kernels for 0%

commit v1 on v0

v1 whole, which is shorter than its diff:
```python
import functools
import math

import jax
import jax.numpy as jnp
from jax import lax
from jax.experimental import pallas as pl
from jax.experimental.pallas import tpu as pltpu
from jax.sharding import PartitionSpec as P

HD = 128
KB = 512
LANES = 128
NEG_FILL = -1e30
TO_LOG2 = math.log2(math.e) / math.sqrt(HD)
VMEM_LIMIT = 40 * 1024 * 1024
PART = 32


def params():
    return pltpu.CompilerParams(vmem_limit_bytes=VMEM_LIMIT)


def lane_iota(shape):
    return lax.broadcasted_iota(jnp.int32, shape, len(shape) - 1)


def pack_body(queries_ref, hits_ref, out_ref):
    own_rows, width = queries_ref.shape
    heads = width // HD
    chips, rows, _ = out_ref.shape
    group_rows = rows - 16 - heads * own_rows
    queries = queries_ref[...].astype(jnp.float32)
    pieces = [queries[:, h * HD:(h + 1) * HD] for h in range(heads)]
    hits = hits_ref[...].astype(jnp.float32)
    hits = jnp.concatenate(
        [hits, jnp.zeros((own_rows, LANES - hits.shape[1]), jnp.float32)], axis=1
    )
    pieces += [hits] * (16 // own_rows)
    message = jnp.concatenate(pieces, axis=0).astype(jnp.bfloat16)
    out_ref[...] = jnp.broadcast_to(message[None], out_ref.shape)


def pack(queries, hits, chips):
    own_rows, width = queries.shape
    rows = width // HD * own_rows + 16
    return pl.pallas_call(
        pack_body,
        out_shape=jax.ShapeDtypeStruct((chips, rows, LANES), jnp.bfloat16),
        compiler_params=params(),
        name="pack_queries",
    )(queries, hits)


def attend_body(kv_heads, q_ref, k_hbm, v_hbm, out_ref, q_buf, k_buf, v_buf, k_sem, v_sem):
    chips, msg_rows, _ = q_ref.shape
    slab = (msg_rows - 16) // kv_heads
    rows = chips * slab
    local_shards, positions, _ = k_hbm.shape
    blocks = positions // KB

    def copies(g):
        columns = pl.ds(g * HD, HD)
        return (
            pltpu.make_async_copy(k_hbm.at[:, :, columns], k_buf.at[g], k_sem.at[g]),
            pltpu.make_async_copy(v_hbm.at[:, :, columns], v_buf.at[g], v_sem.at[g]),
        )

    for g in range(kv_heads):
        for copy in copies(g):
            copy.start()

    for pair in range(kv_heads // 2):
        both = q_ref[:, pair * 2 * slab:(pair + 1) * 2 * slab, :].astype(jnp.float32)
        for i in range(2):
            part = both[:, i * slab:(i + 1) * slab, :].reshape(rows, HD)
            q_buf[pair * 2 + i] = part.astype(jnp.bfloat16)
    listed = q_ref[:, msg_rows - 16:, :].astype(jnp.float32)[:, :slab, :].reshape(rows, LANES)
    first = lax.axis_index("shard") * local_shards
    lane = lane_iota((rows, LANES))
    hit = [
        jnp.sum(jnp.where(lane == first + slot, listed, 0.0), axis=1, keepdims=True) > 0.0
        for slot in range(local_shards)
    ]
    out_ref[kv_heads] = jnp.zeros((rows, LANES), jnp.float32)
    ones = jnp.ones((KB, LANES), jnp.bfloat16)

    def head(g, carry):
        for copy in copies(g):
            copy.wait()
        query = q_buf[g]
        peaks, sums = [], []
        for slot in range(local_shards):
            for block in range(blocks):
                at = slice(block * KB, (block + 1) * KB)
                scores = lax.dot_general(
                    query, k_buf[g, slot, at, :], (((1,), (1,)), ((), ())),
                    preferred_element_type=jnp.float32,
                )
                peak = jnp.max(scores, axis=1, keepdims=True)
                weights = jnp.exp2((scores - peak) * TO_LOG2).astype(jnp.bfloat16)
                values = jnp.concatenate([v_buf[g, slot, at, :], ones], axis=1)
                sums.append(jnp.dot(weights, values, preferred_element_type=jnp.float32))
                peaks.append(jnp.where(hit[slot], peak * TO_LOG2, NEG_FILL))
        top = functools.reduce(jnp.maximum, peaks)
        merged = None
        for i, (peak, total) in enumerate(zip(peaks, sums)):
            factor = jnp.where(hit[i // blocks], jnp.exp2(peak - top), 0.0)
            term = total * factor
            merged = term if merged is None else merged + term
        out_ref[g] = merged[:, :HD]
        stats = out_ref[kv_heads]
        stats = jnp.where(lane == g, top, stats)
        out_ref[kv_heads] = jnp.where(lane == g + PART, merged[:, HD:], stats)
        return carry

    lax.fori_loop(0, kv_heads, head, 0)


def attend(message, keys, values, kv_heads):
    chips, msg_rows, _ = message.shape
    rows = chips * ((msg_rows - 16) // kv_heads)
    local_shards, positions, _ = keys.shape
    cache = pltpu.VMEM((kv_heads, local_shards, positions, HD), keys.dtype)
    return pl.pallas_call(
        functools.partial(attend_body, kv_heads),
        out_shape=jax.ShapeDtypeStruct((kv_heads + 1, rows, LANES), jnp.float32),
        in_specs=[
            pl.BlockSpec(memory_space=pltpu.VMEM),
            pl.BlockSpec(memory_space=pl.ANY),
            pl.BlockSpec(memory_space=pl.ANY),
        ],
        out_specs=pl.BlockSpec(memory_space=pltpu.VMEM),
        scratch_shapes=[
            pltpu.VMEM((kv_heads, rows, HD), jnp.bfloat16),
            cache,
            cache,
            pltpu.SemaphoreType.DMA((kv_heads,)),
            pltpu.SemaphoreType.DMA((kv_heads,)),
        ],
        compiler_params=params(),
        cost_estimate=pl.CostEstimate(
            flops=4 * rows * keys.size,
            bytes_accessed=2 * keys.size * 2,
            transcendentals=rows * keys.size // HD,
        ),
        name="attend",
    )(message, keys, values)


def merge_body(a_ref, b_ref, out_ref):
    kv_heads = a_ref.shape[0] - 1
    rows = a_ref.shape[1]
    chips, msg_rows, _ = out_ref.shape
    slab = rows // chips
    a_stats, b_stats = a_ref[kv_heads], b_ref[kv_heads]
    shift = LANES - PART
    a_total, b_total = pltpu.roll(a_stats, shift, 1), pltpu.roll(b_stats, shift, 1)
    top = jnp.maximum(a_stats, b_stats)
    a_factor, b_factor = jnp.exp2(a_stats - top), jnp.exp2(b_stats - top)
    total = a_total * a_factor + b_total * b_factor
    some = total > 0.0
    safe = jnp.where(some, total, 1.0)
    a_share = jnp.where(some, a_factor / safe, 0.0)
    b_share = jnp.where(some, b_factor / safe, 0.0)
    level = jnp.where(some, top + jnp.log2(safe), NEG_FILL)
    averages = [
        (a_ref[g] * a_share[:, g:g + 1] + b_ref[g] * b_share[:, g:g + 1]).reshape(
            chips, slab, HD
        )
        for g in range(kv_heads)
    ]
    for pair in range(kv_heads // 2):
        both = jnp.concatenate(averages[2 * pair:2 * pair + 2], axis=1)
        out_ref[:, pair * 2 * slab:(pair + 1) * 2 * slab, :] = both.astype(jnp.bfloat16)
    lane = lane_iota((rows, LANES))
    rest = jnp.where(lane < kv_heads, level, 0.0)
    packed = jnp.zeros_like(rest)
    for i in range(3):
        part = rest.astype(jnp.bfloat16).astype(jnp.float32)
        rest = rest - part
        packed = packed + (pltpu.roll(part, PART * i, 1) if i else part)
    packed = packed.reshape(chips, slab, LANES)
    packed = jnp.concatenate([packed] * (16 // slab), axis=1)
    out_ref[:, msg_rows - 16:, :] = packed.astype(jnp.bfloat16)


def merge(a, b, chips):
    kv_heads = a.shape[0] - 1
    msg_rows = kv_heads * (a.shape[1] // chips) + 16
    return pl.pallas_call(
        merge_body,
        out_shape=jax.ShapeDtypeStruct((chips, msg_rows, LANES), jnp.bfloat16),
        compiler_params=params(),
        name="merge_cores",
    )(a, b)


def finish_body(x_ref, out_ref):
    chips, msg_rows, _ = x_ref.shape
    own_rows, width = out_ref.shape
    slab = 8
    kv_heads = (msg_rows - 16) // slab
    stats = x_ref[:, msg_rows - 16:, :].astype(jnp.float32)[:, :slab, :]
    stats = stats.reshape(chips * slab, LANES)
    level = stats
    for i in (1, 2):
        level = level + pltpu.roll(stats, LANES - PART * i, 1)
    level = level.reshape(chips, slab, LANES)
    top = jnp.max(level, axis=0, keepdims=True)
    factor = jnp.exp2(level - top)
    share = factor / jnp.sum(factor, axis=0, keepdims=True)
    pieces = []
    for pair in range(kv_heads // 2):
        both = x_ref[:, pair * 2 * slab:(pair + 1) * 2 * slab, :].astype(jnp.float32)
        for i in range(2):
            g = 2 * pair + i
            part = both[:, i * slab:(i + 1) * slab, :] * share[:, :, g:g + 1]
            part = jnp.sum(part, axis=0)
            pieces += [
                part[r * own_rows:(r + 1) * own_rows, :] for r in range(slab // own_rows)
            ]
    out_ref[...] = jnp.concatenate(pieces, axis=1).astype(jnp.bfloat16)


def finish(received, own_rows, width):
    return pl.pallas_call(
        finish_body,
        out_shape=jax.ShapeDtypeStruct((own_rows, width), jnp.bfloat16),
        compiler_params=params(),
        name="finish",
    )(received)


def shards(devices, queries, cached_keys, cached_values, shard_hits):
    kv_heads = cached_keys.shape[2] // HD
    chips = devices // 2
    axes = ("shard", "seq")
    same_core = [[2 * i + core for i in range(chips)] for core in range(2)]
    siblings = [(i, i ^ 1) for i in range(devices)]
    message = pack(queries, shard_hits, chips)
    own = lax.all_to_all(message, axes, 0, 0, axis_index_groups=same_core)
    other = lax.ppermute(own, axes, siblings)
    own_state = attend(own, cached_keys, cached_values, kv_heads)
    other_state = attend(other, cached_keys, cached_values, kv_heads)
    sibling_state = lax.ppermute(other_state, axes, siblings)
    partial = merge(own_state, sibling_state, chips)
    received = lax.all_to_all(partial, axes, 0, 0, axis_index_groups=same_core)
    return finish(received, *queries.shape)


def solution(mesh):
    both = P(("shard", "seq"), None)
    cache = P("shard", "seq", None)
    return jax.shard_map(
        functools.partial(shards, mesh.size),
        mesh=mesh,
        in_specs=(both, cache, cache, both),
        out_specs=both,
        check_vma=False,
    )
```

time: 307 us -> 60.8 us (0.20)
  blocking collectives: 161 us -> 35.5 us
  waiting for transfers between devices: 94.8 us -> 1.63 us
  Pallas kernels: 0 us -> 17.3 us
  local copies, waits for them, and re-layouts: 20.3 us -> 5.77 us
  between operations: 13.5 us -> 0.04 us
  matrix products: 8.4 us -> 0 us
  other arithmetic: 7.78 us -> 0 us
    reduce_scatter x1 -> x0, waiting for transfers between devices: 94.7 us -> none  [shards(): lax.psum_scatter(numerator * factor[..., None], ('shard', 'seq'), scatter...]
    all_gather x2 -> x0, blocking collectives: 82.6 us -> none  [the longest x1 43.5 us: shards(): lax.all_gather(shard_hits, ('shard', 'seq'), axis=0, tiled=True)]
    pmax x1 -> x0, blocking collectives: 39.4 us -> none  [shards(): lax.pmax(maximum.astype(jnp.bfloat16), ('shard', 'seq'))]
    unnamed x1 -> x0, blocking collectives: 39.2 us -> none
    all_to_all x0 -> x2, blocking collectives: none -> 35.5 us  [the longest x1 20.1 us: shards(): own = lax.all_to_all(message, axes, 0, 0, axis_index_groups=same_core)]
    pallas_call x0 -> x5, Pallas kernels: none -> 17.3 us  [the longest x2 15.9 us: attend(): pl.pallas_call(functools.partial(attend_body, kv_heads), out_shape=jax.Sh...]
    dot_general x8 -> x0, matrix products: 8.4 us -> none  [the longest x4 5.2 us: advance(): jnp.einsum('ngrt,tgd->ngrd', weights, value_block, preferred_element_type...]
    unnamed x13 -> x10, local copies, waits for them, and re-layouts: 13.1 us -> 5.77 us
  transfers between devices with their start and end apart: 1 -> 2, of which waited for: 1 -> 1; matrix products, arithmetic and copies ran while one was open for 0% -> 0% of each run, Pallas kernels for 0% -> 13%
where the time goes in v1:
time: 60.8 us; the launch traced here: 60.5 us
  blocking collectives  35.5 us (58%)
  Pallas kernels  17.3 us (28%)
  local copies, waits for them, and re-layouts  5.77 us (9%)
  waiting for transfers between devices  1.63 us (3%)
    all_to_all x1, blocking collectives, shards(): own = lax.all_to_all(message, axes, 0, 0, axis_index_groups=same_core)  20.1 us
    pallas_call x2, Pallas kernels, attend(): pl.pallas_call(functools.partial(attend_body, kv_heads), out_shape=jax.Sh...  15.9 us
    all_to_all x1, blocking collectives, shards(): received = lax.all_to_all(partial, axes, 0, 0, axis_index_groups=same_core)  15.4 us
    unnamed x10, local copies, waits for them, and re-layouts  5.77 us
    ppermute x1, waiting for transfers between devices, shards(): other = lax.ppermute(own, axes, siblings)  1.63 us
  transfers between devices with their start and end apart: 2, of which 1 were waited for; matrix products, arithmetic and copies ran while one was open for 0% of the time, Pallas kernels for 13%

profile of v1, /device:TPU:0, one launch (start us, length us, event | category | flops | bytes accessed | tf_op | source)
XLA Modules:
  0.0 60.5 jit_solution(3511612920819131112)
XLA Ops:
  0.0 0.0 copy-start.3
  0.0 0.7 %copy-done.3 = bf16[2,4096]{1,0:T(2,128)(2,1)S(1)} copy-done((bf16[2,4096]{1,0:T(2,128)(2,1)S(1)}, bf16[2,4096]{1,0:T(2,128)(2,1)}, u32[]{:S(2)}) %copy-start.3) | copy-done | bytes 16408
  0.7 0.0 copy-start.4
  0.7 0.7 %copy-done.4 = s32[2,8]{1,0:T(2,128)S(1)} copy-done((s32[2,8]{1,0:T(2,128)S(1)}, s32[2,8]{1,0:T(2,128)}, u32[]{:S(2)}) %copy-start.4) | copy-done | bytes 88
  1.4 20.1 %all_to_all.10.q_ref = bf16[16,80,128]{2,1,0:T(8,128)(2,1)S(1)} all-to-all(bf16[16,80,128]{2,1,0:T(8,128)(2,1)S(1)} %pack_queries.1), channel_id=1, replica_groups={{0,2,4,6,8,10,12,14,16,18,20,22,24,26,28,30},{1,3,5,7,9,11,13,15,17,19,..., dimensions={0} | all-to-all | bytes 655360 | tf_op jit(solution)/shard_map/all_to_all | solution.py:242
  21.5 0.0 collective-permute-start
  21.5 1.6 %collective-permute-done.q_ref = bf16[16,80,128]{2,1,0:T(8,128)(2,1)S(1)} collective-permute-done((bf16[16,80,128]{2,1,0:T(8,128)(2,1)S(1)}, bf16[16,80,128]{2,1,0:T(8,128)(2,1)S(1)}, u32[]{:S(2)}, u32[]{:S(2)}) %collective-permute-start) | collective-permute-done | bytes 327712 | tf_op jit(solution)/shard_map/ppermute | solution.py:243
  23.2 0.0 copy-start
  23.2 2.2 %copy-done = bf16[2,1024,1024]{2,1,0:T(8,128)(2,1)S(1)} copy-done((bf16[2,1024,1024]{2,1,0:T(8,128)(2,1)S(1)}, bf16[2,1024,1024]{2,1,0:T(8,128)(2,1)}, u32[]{:S(2)}) %copy-start) | copy-done | bytes 4194328
  25.3 0.0 copy-start.2
  25.3 2.2 %copy-done.2 = bf16[2,1024,1024]{2,1,0:T(8,128)(2,1)S(1)} copy-done((bf16[2,1024,1024]{2,1,0:T(8,128)(2,1)S(1)}, bf16[2,1024,1024]{2,1,0:T(8,128)(2,1)}, u32[]{:S(2)}) %copy-start.2) | copy-done | bytes 4194328
  27.5 0.0 copy-start.1
  27.5 7.9 %attend.3 = f32[9,128,128]{2,1,0:T(8,128)S(1)} custom-call(bf16[16,80,128]{2,1,0:T(8,128)(2,1)S(1)} %collective-permute-done.q_ref, bf16[2,1024,1024]{2,1,0:T(8,128)(2,1)S(1)} %copy-done, bf16[2,1024,1024]{2,1,0:T(8,128)(2,1)S(1)} %copy-done.2), custom_call_target="tpu_custom_call" | custom-call | flops 1073741824 | bytes 8388608 | tf_op jit(solution)/shard_map/attend/pallas_call | solution.py:125
  35.5 0.2 collective-permute-start.1
  35.7 0.0 copy-done.1
  35.7 8.0 %attend.2.a_ref = f32[9,128,128]{2,1,0:T(8,128)S(1)} custom-call(bf16[16,80,128]{2,1,0:T(8,128)(2,1)S(1)} %all_to_all.10.q_ref, bf16[2,1024,1024]{2,1,0:T(8,128)(2,1)S(1)} %copy-done.1, bf16[2,1024,1024]{2,1,0:T(8,128)(2,1)S(1)} %copy-done.2), custom_call_target="tpu_custom_call" | custom-call | flops 1073741824 | bytes 8388608 | tf_op jit(solution)/shard_map/attend/pallas_call | solution.py:125
  43.6 0.0 collective-permute-done.1.b_ref
  43.7 0.5 merge_cores.1
  44.1 15.4 %all_to_all.11.x_ref = bf16[16,80,128]{2,1,0:T(8,128)(2,1)S(1)} all-to-all(bf16[16,80,128]{2,1,0:T(8,128)(2,1)S(1)} %merge_cores.1), channel_id=1, replica_groups={{0,2,4,6,8,10,12,14,16,18,20,22,24,26,28,30},{1,3,5,7,9,11,13,15,17,19,..., dimensions={0} | all-to-all | bytes 655360 | tf_op jit(solution)/shard_map/all_to_all | solution.py:248
  59.5 1.0 %finish.1 = bf16[2,4096]{1,0:T(2,128)(2,1)} custom-call(bf16[16,80,128]{2,1,0:T(8,128)(2,1)S(1)} %all_to_all.11.x_ref), custom_call_target="tpu_custom_call" | custom-call | tf_op jit(solution)/shard_map/finish/pallas_call | solution.py:227
  (1 shorter events, 0.0 us)
Async XLA Ops:
  0.0 0.7 %copy-start.3 = (bf16[2,4096]{1,0:T(2,128)(2,1)S(1)}, bf16[2,4096]{1,0:T(2,128)(2,1)}, u32[]{:S(2)}) copy-start(bf16[2,4096]{1,0:T(2,128)(2,1)} %queries_ref.1) | copy-start | bytes 49156
  0.7 0.7 %copy-start.4 = (s32[2,8]{1,0:T(2,128)S(1)}, s32[2,8]{1,0:T(2,128)}, u32[]{:S(2)}) copy-start(s32[2,8]{1,0:T(2,128)} %hits_ref.1) | copy-start | bytes 196
  21.5 1.6 %collective-permute-start = (bf16[16,80,128]{2,1,0:T(8,128)(2,1)S(1)}, bf16[16,80,128]{2,1,0:T(8,128)(2,1)S(1)}, u32[]{:S(2)}, u32[]{:S(2)}) collective-permute-start(bf16[16,80,128]{2,1,0:T(8,128)(2,1)S(1)} %all_to_all.10.q_ref), channel_id=1, source_target_pairs={{0,1},{1,0},{2,3},{3,2},{4,5},{5,4},{6,7},{7,6},{8,9},{9,8},{10,11... | collective-permute-start | bytes 983048 | tf_op jit(solution)/shard_map/ppermute | solution.py:243
  23.2 2.2 %copy-start = (bf16[2,1024,1024]{2,1,0:T(8,128)(2,1)S(1)}, bf16[2,1024,1024]{2,1,0:T(8,128)(2,1)}, u32[]{:S(2)}) copy-start(bf16[2,1024,1024]{2,1,0:T(8,128)(2,1)} %k_hbm.3) | copy-start | bytes 12582916
  25.3 2.2 %copy-start.2 = (bf16[2,1024,1024]{2,1,0:T(8,128)(2,1)S(1)}, bf16[2,1024,1024]{2,1,0:T(8,128)(2,1)}, u32[]{:S(2)}) copy-start(bf16[2,1024,1024]{2,1,0:T(8,128)(2,1)} %v_hbm.3) | copy-start | bytes 12582916
  27.5 8.1 %copy-start.1 = (bf16[2,1024,1024]{2,1,0:T(8,128)(2,1)S(1)}, bf16[2,1024,1024]{2,1,0:T(8,128)(2,1)}, u32[]{:S(2)}) copy-start(bf16[2,1024,1024]{2,1,0:T(8,128)(2,1)} %k_hbm.3) | copy-start | bytes 12582916
  35.5 8.2 %collective-permute-start.1 = (f32[9,128,128]{2,1,0:T(8,128)S(1)}, f32[9,128,128]{2,1,0:T(8,128)S(1)}, u32[]{:S(2)}, u32[]{:S(2)}) collective-permute-start(f32[9,128,128]{2,1,0:T(8,128)S(1)} %attend.3), channel_id=1, source_target_pairs={{0,1},{1,0},{2,3},{3,2},{4,5},{5,4},{6,7},{7,6},{8,9},{9,8},{10,11... | collective-permute-start | bytes 1769480 | tf_op jit(solution)/shard_map/ppermute | solution.py:246

commit v2 on v1

v2 whole, which is shorter than its diff:
```python
import functools
import math

import jax
import jax.numpy as jnp
from jax import lax
from jax.experimental import pallas as pl
from jax.experimental.pallas import tpu as pltpu
from jax.sharding import PartitionSpec as P

HD = 128
KB = 512
LANES = 128
NEG_FILL = -1e30
TO_LOG2 = math.log2(math.e) / math.sqrt(HD)
PACK_COST = 20_000_000_000
VMEM_LIMIT = 40 * 1024 * 1024
PART = 32
SLAB = 8


def params():
    return pltpu.CompilerParams(vmem_limit_bytes=VMEM_LIMIT)


def lane_iota(shape):
    return lax.broadcasted_iota(jnp.int32, shape, len(shape) - 1)


def pack_body(queries_ref, hits_ref, out_ref):
    own_rows, width = queries_ref.shape
    heads = width // HD
    queries = queries_ref[...].astype(jnp.float32)
    pieces = [queries[:, h * HD:(h + 1) * HD] for h in range(heads)]
    hits = hits_ref[...].astype(jnp.float32)
    hits = jnp.concatenate(
        [hits, jnp.zeros((own_rows, LANES - hits.shape[1]), jnp.float32)], axis=1
    )
    pieces += [hits] * (SLAB // own_rows)
    message = jnp.concatenate(pieces, axis=0).astype(jnp.bfloat16)
    out_ref[...] = jnp.broadcast_to(message[None], out_ref.shape)


def pack(queries, hits, chips):
    own_rows, width = queries.shape
    rows = width // HD * own_rows + SLAB
    return pl.pallas_call(
        pack_body,
        out_shape=jax.ShapeDtypeStruct((chips, rows, LANES), jnp.bfloat16),
        compiler_params=params(),
        cost_estimate=pl.CostEstimate(flops=PACK_COST, bytes_accessed=0, transcendentals=0),
        name="pack_queries",
    )(queries, hits)


def rows_of(ref, g, slab):
    chips = ref.shape[0]
    pair = ref[:, (g // 2) * 2 * slab:(g // 2 + 1) * 2 * slab, :].astype(jnp.float32)
    at = (g % 2) * slab
    return pair[:, at:at + slab, :].reshape(chips * slab, LANES)


def one_hot(condition):
    return jnp.where(condition, 1.0, 0.0).astype(jnp.bfloat16)


def two_parts(x):
    high = x.astype(jnp.bfloat16)
    return high, (x - high.astype(jnp.float32)).astype(jnp.bfloat16)


def attend_body(own_rows, own_ref, other_ref, k_ref, v_ref, own_out, other_out, q_buf, y_buf):
    chips, msg_rows, _ = own_ref.shape
    slab = SLAB
    kv_heads = msg_rows // slab - 1
    group = slab // own_rows
    rows = chips * slab
    local_shards, positions, _ = k_ref.shape
    blocks = positions // KB
    cap = 2 * chips * own_rows // 2
    packed = group * cap
    both = 2 * rows

    listed = jnp.concatenate(
        [
            ref[:, msg_rows - slab:, :].astype(jnp.float32).reshape(rows, LANES)
            for ref in (own_ref, other_ref)
        ],
        axis=0,
    )
    first = lax.axis_index("shard") * local_shards
    lane = lane_iota((both, LANES))
    slots = jnp.zeros((both, LANES), jnp.float32)
    for slot in range(local_shards):
        hit = jnp.sum(jnp.where(lane == first + slot, listed, 0.0), axis=1, keepdims=True)
        slots = jnp.where(lane == slot, hit, slots)

    def query_of(at):
        return lax.div(at, slab) * own_rows + lax.rem(at, own_rows)

    def head_of(at):
        return lax.div(lax.rem(at, slab), own_rows)

    row_query = query_of(lax.broadcasted_iota(jnp.int32, (both, both), 0))
    col_query = query_of(lax.broadcasted_iota(jnp.int32, (both, both), 1))
    earlier = one_hot(col_query < row_query)
    place = jnp.dot(earlier, slots.astype(jnp.bfloat16), preferred_element_type=jnp.float32)
    slots_t = jnp.transpose(slots)[:8]
    later = one_hot(row_query < col_query)
    place_t = jnp.dot(slots_t.astype(jnp.bfloat16), later, preferred_element_type=jnp.float32)

    def packed_key(at):
        return lax.div(at, cap), (lax.rem(at, cap) * group).astype(jnp.float32)

    pick_head, pick_place = packed_key(lax.broadcasted_iota(jnp.int32, (packed, both), 0))
    pick_from = head_of(lax.broadcasted_iota(jnp.int32, (packed, both), 1))
    back_head, back_place = packed_key(lax.broadcasted_iota(jnp.int32, (both, packed), 1))
    back_from = head_of(lax.broadcasted_iota(jnp.int32, (both, packed), 0))
    back = []
    queries = [
        jnp.concatenate([rows_of(own_ref, g, slab), rows_of(other_ref, g, slab)], axis=0)
        for g in range(kv_heads)
    ]
    queries = jnp.concatenate(queries, axis=1).astype(jnp.bfloat16)
    for slot in range(local_shards):
        pick = one_hot(
            (pick_head == pick_from)
            & (pick_place == place_t[slot:slot + 1])
            & (slots_t[slot:slot + 1] > 0.0)
        )
        q_buf[slot] = jnp.dot(pick, queries, preferred_element_type=jnp.float32).astype(
            jnp.bfloat16
        )
        back.append(
            one_hot(
                (back_head == back_from)
                & (back_place == place[:, slot:slot + 1])
                & (slots[:, slot:slot + 1] > 0.0)
            )
        )

    ones = jnp.ones((KB, LANES), jnp.bfloat16)
    peak_of = []
    for slot in range(local_shards):
        tops = []
        for g in range(kv_heads):
            columns = slice(g * HD, (g + 1) * HD)
            query = q_buf[slot, :, columns]
            peaks, sums = [], []
            for block in range(blocks):
                at = slice(block * KB, (block + 1) * KB)
                scores = lax.dot_general(
                    k_ref[slot, at, columns], query, (((1,), (1,)), ((), ())),
                    preferred_element_type=jnp.float32,
                )
                peak = jnp.max(scores, axis=0, keepdims=True)
                weights = jnp.exp2((scores - peak) * TO_LOG2).astype(jnp.bfloat16)
                values = jnp.concatenate([v_ref[slot, at, columns], ones], axis=1)
                sums.append(
                    lax.dot_general(
                        weights, values, (((0,), (0,)), ((), ())),
                        preferred_element_type=jnp.float32,
                    )
                )
                peaks.append(peak * TO_LOG2)
            top = functools.reduce(jnp.maximum, peaks)
            factors = [jnp.exp2(peak - top) for peak in peaks]
            factors.append(jnp.zeros((8 - len(factors), packed), jnp.float32))
            factors = jnp.transpose(jnp.concatenate(factors, axis=0))
            total = sum(part * factors[:, i:i + 1] for i, part in enumerate(sums))
            high, low = two_parts(total)
            y_buf[slot, g] = jnp.concatenate([high, low], axis=0)
            tops.append(top)
        rest = jnp.concatenate(tops + [jnp.zeros_like(tops[0])] * (16 - kv_heads), axis=0)
        parts = []
        for _ in range(3):
            part = rest.astype(jnp.bfloat16)
            parts.append(part)
            rest = rest - part.astype(jnp.float32)
        peak = lax.dot_general(
            jnp.concatenate([back[slot]] * 3, axis=1), jnp.concatenate(parts, axis=1),
            (((1,), (1,)), ((), ())), preferred_element_type=jnp.float32,
        )
        peak_of.append(jnp.where(slots[:, slot:slot + 1] > 0.0, peak, NEG_FILL))

    top = functools.reduce(jnp.maximum, peak_of)
    factor_of = [jnp.where(peak > NEG_FILL, jnp.exp2(peak - top), 0.0) for peak in peak_of]
    twice = [jnp.concatenate([one] * 2, axis=1) for one in back]
    stats = jnp.zeros((both, LANES), jnp.float32)
    for g in range(kv_heads):
        total = None
        for slot in range(local_shards):
            term = jnp.dot(twice[slot], y_buf[slot, g], preferred_element_type=jnp.float32)
            term = term * factor_of[slot][:, g:g + 1]
            total = term if total is None else total + term
        own_out[g] = total[:rows, :HD]
        other_out[g] = total[rows:, :HD]
        stats = jnp.where(lane == g, top[:, g:g + 1], stats)
        stats = jnp.where(lane == g + PART, total[:, HD:], stats)
    own_out[kv_heads] = stats[:rows]
    other_out[kv_heads] = stats[rows:]


def attend(own, other, keys, values, own_rows):
    chips, msg_rows, _ = own.shape
    kv_heads = msg_rows // SLAB - 1
    rows = chips * SLAB
    packed = SLAB // own_rows * chips * own_rows
    local_shards = keys.shape[0]
    state = jax.ShapeDtypeStruct((kv_heads + 1, rows, LANES), jnp.float32)
    return pl.pallas_call(
        functools.partial(attend_body, own_rows),
        out_shape=(state, state),
        scratch_shapes=[
            pltpu.VMEM((local_shards, packed, kv_heads * HD), jnp.bfloat16),
            pltpu.VMEM((local_shards, kv_heads, 2 * packed, 2 * LANES), jnp.bfloat16),
        ],
        compiler_params=params(),
        cost_estimate=pl.CostEstimate(
            flops=4 * packed * keys.size,
            bytes_accessed=2 * keys.size * 2,
            transcendentals=packed * keys.size // HD,
        ),
        name="attend",
    )(own, other, keys, values)


def merge_body(a_ref, b_ref, out_ref):
    kv_heads = a_ref.shape[0] - 1
    rows = a_ref.shape[1]
    chips, msg_rows, _ = out_ref.shape
    slab = rows // chips
    a_stats, b_stats = a_ref[kv_heads], b_ref[kv_heads]
    shift = LANES - PART
    a_total, b_total = pltpu.roll(a_stats, shift, 1), pltpu.roll(b_stats, shift, 1)
    top = jnp.maximum(a_stats, b_stats)
    a_factor, b_factor = jnp.exp2(a_stats - top), jnp.exp2(b_stats - top)
    total = a_total * a_factor + b_total * b_factor
    some = total > 0.0
    safe = jnp.where(some, total, 1.0)
    a_share = jnp.where(some, a_factor / safe, 0.0)
    b_share = jnp.where(some, b_factor / safe, 0.0)
    level = jnp.where(some, top + jnp.log2(safe), NEG_FILL)
    averages = [
        (a_ref[g] * a_share[:, g:g + 1] + b_ref[g] * b_share[:, g:g + 1]).reshape(
            chips, slab, HD
        )
        for g in range(kv_heads)
    ]
    for pair in range(kv_heads // 2):
        both = jnp.concatenate(averages[2 * pair:2 * pair + 2], axis=1)
        out_ref[:, pair * 2 * slab:(pair + 1) * 2 * slab, :] = both.astype(jnp.bfloat16)
    lane = lane_iota((rows, LANES))
    rest = jnp.where(lane < kv_heads, level, 0.0)
    packed = jnp.zeros_like(rest)
    for i in range(3):
        part = rest.astype(jnp.bfloat16).astype(jnp.float32)
        rest = rest - part
        packed = packed + (pltpu.roll(part, PART * i, 1) if i else part)
    out_ref[:, msg_rows - slab:, :] = packed.reshape(chips, slab, LANES).astype(jnp.bfloat16)


def merge(a, b, chips):
    kv_heads = a.shape[0] - 1
    msg_rows = (kv_heads + 1) * SLAB
    return pl.pallas_call(
        merge_body,
        out_shape=jax.ShapeDtypeStruct((chips, msg_rows, LANES), jnp.bfloat16),
        compiler_params=params(),
        name="merge_cores",
    )(a, b)


def finish_body(x_ref, out_ref):
    chips, msg_rows, _ = x_ref.shape
    own_rows, width = out_ref.shape
    slab = SLAB
    kv_heads = msg_rows // slab - 1
    stats = x_ref[:, msg_rows - slab:, :].astype(jnp.float32).reshape(chips * slab, LANES)
    level = stats
    for i in (1, 2):
        level = level + pltpu.roll(stats, LANES - PART * i, 1)
    level = level.reshape(chips, slab, LANES)
    top = jnp.max(level, axis=0, keepdims=True)
    factor = jnp.exp2(level - top)
    share = factor / jnp.sum(factor, axis=0, keepdims=True)
    pieces = []
    for pair in range(kv_heads // 2):
        both = x_ref[:, pair * 2 * slab:(pair + 1) * 2 * slab, :].astype(jnp.float32)
        for i in range(2):
            g = 2 * pair + i
            part = both[:, i * slab:(i + 1) * slab, :] * share[:, :, g:g + 1]
            part = jnp.sum(part, axis=0)
            pieces += [
                part[r * own_rows:(r + 1) * own_rows, :] for r in range(slab // own_rows)
            ]
    out_ref[...] = jnp.concatenate(pieces, axis=1).astype(jnp.bfloat16)


def finish(received, own_rows, width):
    return pl.pallas_call(
        finish_body,
        out_shape=jax.ShapeDtypeStruct((own_rows, width), jnp.bfloat16),
        compiler_params=params(),
        name="finish",
    )(received)


def shards(devices, queries, cached_keys, cached_values, shard_hits):
    chips = devices // 2
    axes = ("shard", "seq")
    same_core = [[2 * i + core for i in range(chips)] for core in range(2)]
    siblings = [(i, i ^ 1) for i in range(devices)]
    message = pack(queries, shard_hits, chips)
    own = lax.all_to_all(message, axes, 0, 0, axis_index_groups=same_core)
    other = lax.ppermute(own, axes, siblings)
    own_state, other_state = attend(own, other, cached_keys, cached_values, queries.shape[0])
    sibling_state = lax.ppermute(other_state, axes, siblings)
    partial = merge(own_state, sibling_state, chips)
    received = lax.all_to_all(partial, axes, 0, 0, axis_index_groups=same_core)
    return finish(received, *queries.shape)


def solution(mesh):
    both = P(("shard", "seq"), None)
    cache = P("shard", "seq", None)
    return jax.shard_map(
        functools.partial(shards, mesh.size),
        mesh=mesh,
        in_specs=(both, cache, cache, both),
        out_specs=both,
        check_vma=False,
    )
```

time: 60.8 us -> 47 us (0.77)
  Pallas kernels: 17.3 us -> 7.13 us
  local copies, waits for them, and re-layouts: 5.77 us -> 1.75 us
  waiting for transfers between devices: 1.63 us -> 3.45 us
  blocking collectives: 35.5 us -> 34.1 us
    pallas_call x2 -> x1, Pallas kernels: 15.9 us -> 5.68 us  [attend(): pl.pallas_call(functools.partial(attend_body, own_rows), out_shape=(state...]
    unnamed x10 -> x8, local copies, waits for them, and re-layouts: 5.77 us -> 1.75 us
    ppermute x1, waiting for transfers between devices: 0.01 us -> 1.87 us  [shards(): sibling_state = lax.ppermute(other_state, axes, siblings)]
    all_to_all x1, blocking collectives: 15.4 us -> 14.5 us  [shards(): received = lax.all_to_all(partial, axes, 0, 0, axis_index_groups=same_core)]
  transfers between devices with their start and end apart: 2 -> 2, of which waited for: 1 -> 2; matrix products, arithmetic and copies ran while one was open for 0% -> 0% of each run, Pallas kernels for 13% -> 0%
where the time goes in v2:
time: 47 us; the launch traced here: 46.7 us
  blocking collectives  34.1 us (73%)
  Pallas kernels  7.13 us (15%)
  waiting for transfers between devices  3.45 us (7%)
  local copies, waits for them, and re-layouts  1.75 us (4%)
    all_to_all x1, blocking collectives, shards(): own = lax.all_to_all(message, axes, 0, 0, axis_index_groups=same_core)  19.7 us
    all_to_all x1, blocking collectives, shards(): received = lax.all_to_all(partial, axes, 0, 0, axis_index_groups=same_core)  14.5 us
    pallas_call x1, Pallas kernels, attend(): pl.pallas_call(functools.partial(attend_body, own_rows), out_shape=(state...  5.68 us
    ppermute x1, waiting for transfers between devices, shards(): sibling_state = lax.ppermute(other_state, axes, siblings)  1.87 us
    unnamed x8, local copies, waits for them, and re-layouts  1.75 us
    ppermute x1, waiting for transfers between devices, shards(): other = lax.ppermute(own, axes, siblings)  1.58 us
    pallas_call x1, Pallas kernels, finish(): pl.pallas_call(finish_body, out_shape=jax.ShapeDtypeStruct((own_rows, wid...  0.96 us
  transfers between devices with their start and end apart: 2, of which 2 were waited for; matrix products, arithmetic and copies ran while one was open for 0% of the time, Pallas kernels for 0%

profile of v2, /device:TPU:0, one launch (start us, length us, event | category | flops | bytes accessed | tf_op | source)
XLA Modules:
  0.0 46.7 jit_solution(7110085359997481304)
XLA Ops:
  0.0 0.0 copy-start.1
  0.0 0.0 copy-start.2
  0.0 0.9 %copy-done.2 = bf16[2,4096]{1,0:T(2,128)(2,1)S(1)} copy-done((bf16[2,4096]{1,0:T(2,128)(2,1)S(1)}, bf16[2,4096]{1,0:T(2,128)(2,1)}, u32[]{:S(2)}) %copy-start.2) | copy-done | bytes 16408
  0.9 0.0 copy-start.3
  0.9 0.9 %copy-done.3 = s32[2,8]{1,0:T(2,128)S(1)} copy-done((s32[2,8]{1,0:T(2,128)S(1)}, s32[2,8]{1,0:T(2,128)}, u32[]{:S(2)}) %copy-start.3) | copy-done | bytes 88
  1.8 0.0 copy-start
  1.8 19.7 %all_to_all.10.own_ref = bf16[16,72,128]{2,1,0:T(8,128)(2,1)S(1)} all-to-all(bf16[16,72,128]{2,1,0:T(8,128)(2,1)S(1)} %pack_queries.1), channel_id=1, replica_groups={{0,2,4,6,8,10,12,14,16,18,20,22,24,26,28,30},{1,3,5,7,9,11,13,15,17,19,..., dimensions={0} | all-to-all | bytes 589824 | tf_op jit(solution)/shard_map/all_to_all | solution.py:315
  21.4 0.0 collective-permute-start
  21.4 1.6 %collective-permute-done.other_ref = bf16[16,72,128]{2,1,0:T(8,128)(2,1)S(1)} collective-permute-done((bf16[16,72,128]{2,1,0:T(8,128)(2,1)S(1)}, bf16[16,72,128]{2,1,0:T(8,128)(2,1)S(1)}, u32[]{:S(2)}, u32[]{:S(2)}) %collective-permute-start) | collective-permute-done | bytes 294944 | tf_op jit(solution)/shard_map/ppermute | solution.py:316
  23.0 0.0 copy-done.1
  23.0 0.0 copy-done
  23.0 5.7 %attend.1 = (f32[9,128,128]{2,1,0:T(8,128)S(1)}, f32[9,128,128]{2,1,0:T(8,128)S(1)}) custom-call(bf16[16,72,128]{2,1,0:T(8,128)(2,1)S(1)} %all_to_all.10.own_ref, bf16[16,72,128]{2,1,0:T(8,128)(2,1)S(1)} %collective-permute-done.other_ref, bf16[2,1024,1024]{2,1,0:T(8,128)(2,1)S(1)} %copy-done, bf16[2,1024,1024]{2,1,0:T(8,128)(2,1)S(1)} %copy-done.1), custom_call_target="tpu_custom_call" | custom-call | flops 1073741824 | bytes 8388608 | tf_op jit(solution)/shard_map/attend/pallas_call | solution.py:211
  28.7 0.2 collective-permute-start.1
  28.9 1.9 %collective-permute-done.1.b_ref = f32[9,128,128]{2,1,0:T(8,128)S(1)} collective-permute-done((f32[9,128,128]{2,1,0:T(8,128)S(1)}, f32[9,128,128]{2,1,0:T(8,128)S(1)}, u32[]{:S(2)}, u32[]{:S(2)}) %collective-permute-start.1) | collective-permute-done | bytes 589856 | tf_op jit(solution)/shard_map/ppermute | solution.py:318
  30.8 0.5 %merge_cores.1 = bf16[16,72,128]{2,1,0:T(8,128)(2,1)S(1)} custom-call(f32[9,128,128]{2,1,0:T(8,128)S(1)} %get-tuple-element.7.a_ref, f32[9,128,128]{2,1,0:T(8,128)S(1)} %collective-permute-done.1.b_ref), custom_call_target="tpu_custom_call" | custom-call | tf_op jit(solution)/shard_map/merge_cores/pallas_call | solution.py:266
  31.3 14.5 %all_to_all.11.x_ref = bf16[16,72,128]{2,1,0:T(8,128)(2,1)S(1)} all-to-all(bf16[16,72,128]{2,1,0:T(8,128)(2,1)S(1)} %merge_cores.1), channel_id=1, replica_groups={{0,2,4,6,8,10,12,14,16,18,20,22,24,26,28,30},{1,3,5,7,9,11,13,15,17,19,..., dimensions={0} | all-to-all | bytes 589824 | tf_op jit(solution)/shard_map/all_to_all | solution.py:320
  45.7 1.0 %finish.1 = bf16[2,4096]{1,0:T(2,128)(2,1)} custom-call(bf16[16,72,128]{2,1,0:T(8,128)(2,1)S(1)} %all_to_all.11.x_ref), custom_call_target="tpu_custom_call" | custom-call | tf_op jit(solution)/shard_map/finish/pallas_call | solution.py:301
  (1 shorter events, 0.0 us)
Async XLA Ops:
  0.0 23.0 %copy-start.1 = (bf16[2,1024,1024]{2,1,0:T(8,128)(2,1)S(1)}, bf16[2,1024,1024]{2,1,0:T(8,128)(2,1)}, u32[]{:S(2)}) copy-start(bf16[2,1024,1024]{2,1,0:T(8,128)(2,1)} %v_ref.1) | copy-start | bytes 12582916
  0.0 0.9 %copy-start.2 = (bf16[2,4096]{1,0:T(2,128)(2,1)S(1)}, bf16[2,4096]{1,0:T(2,128)(2,1)}, u32[]{:S(2)}) copy-start(bf16[2,4096]{1,0:T(2,128)(2,1)} %queries_ref.1) | copy-start | bytes 49156
  0.9 0.9 %copy-start.3 = (s32[2,8]{1,0:T(2,128)S(1)}, s32[2,8]{1,0:T(2,128)}, u32[]{:S(2)}) copy-start(s32[2,8]{1,0:T(2,128)} %hits_ref.1) | copy-start | bytes 196
  1.8 21.3 %copy-start = (bf16[2,1024,1024]{2,1,0:T(8,128)(2,1)S(1)}, bf16[2,1024,1024]{2,1,0:T(8,128)(2,1)}, u32[]{:S(2)}) copy-start(bf16[2,1024,1024]{2,1,0:T(8,128)(2,1)} %k_ref.1) | copy-start | bytes 12582916
  21.4 1.6 %collective-permute-start = (bf16[16,72,128]{2,1,0:T(8,128)(2,1)S(1)}, bf16[16,72,128]{2,1,0:T(8,128)(2,1)S(1)}, u32[]{:S(2)}, u32[]{:S(2)}) collective-permute-start(bf16[16,72,128]{2,1,0:T(8,128)(2,1)S(1)} %all_to_all.10.own_ref), channel_id=1, source_target_pairs={{0,1},{1,0},{2,3},{3,2},{4,5},{5,4},{6,7},{7,6},{8,9},{9,8},{10,11... | collective-permute-start | bytes 884744 | tf_op jit(solution)/shard_map/ppermute | solution.py:316
  28.7 2.1 %collective-permute-start.1 = (f32[9,128,128]{2,1,0:T(8,128)S(1)}, f32[9,128,128]{2,1,0:T(8,128)S(1)}, u32[]{:S(2)}, u32[]{:S(2)}) collective-permute-start(f32[9,128,128]{2,1,0:T(8,128)S(1)} %get-tuple-element.8), channel_id=1, source_target_pairs={{0,1},{1,0},{2,3},{3,2},{4,5},{5,4},{6,7},{7,6},{8,9},{9,8},{10,11... | collective-permute-start | bytes 1769480 | tf_op jit(solution)/shard_map/ppermute | solution.py:318

commit v3 on v2

v3 whole, which is shorter than its diff:
```python
import functools
import math

import jax
import jax.numpy as jnp
from jax import lax
from jax.experimental import pallas as pl
from jax.experimental.pallas import tpu as pltpu
from jax.sharding import PartitionSpec as P

HD = 128
KB = 512
LANES = 128
NEG_FILL = -1e30
TO_LOG2 = math.log2(math.e) / math.sqrt(HD)
PACK_COST = 20_000_000_000
VMEM_LIMIT = 24 * 1024 * 1024
PART = 32
SLAB = 8


def params():
    return pltpu.CompilerParams(vmem_limit_bytes=VMEM_LIMIT)


def lane_iota(shape):
    return lax.broadcasted_iota(jnp.int32, shape, len(shape) - 1)


def pack_body(queries_hbm, hits_hbm, out_ref, queries_buf, hits_buf, sems):
    copies = [
        pltpu.make_async_copy(queries_hbm, queries_buf, sems.at[0]),
        pltpu.make_async_copy(hits_hbm, hits_buf, sems.at[1]),
    ]
    for copy in copies:
        copy.start()
    for copy in copies:
        copy.wait()
    own_rows, width = queries_buf.shape
    heads = width // HD
    queries = queries_buf[...].astype(jnp.float32)
    pieces = [queries[:, h * HD:(h + 1) * HD] for h in range(heads)]
    hits = hits_buf[...].astype(jnp.float32)
    hits = jnp.concatenate(
        [hits, jnp.zeros((own_rows, LANES - hits.shape[1]), jnp.float32)], axis=1
    )
    slab = [hits] * (SLAB // own_rows)
    half = heads // 2
    messages = jnp.stack(
        [
            jnp.concatenate(pieces[core * half:(core + 1) * half] + slab, axis=0)
            for core in range(2)
        ]
    ).astype(jnp.bfloat16)
    out_ref[...] = jnp.broadcast_to(messages[None], out_ref.shape)


def pack(queries, hits, devices):
    own_rows, width = queries.shape
    rows = width // HD // 2 * own_rows + SLAB
    out = pl.pallas_call(
        pack_body,
        out_shape=jax.ShapeDtypeStruct((devices // 2, 2, rows, LANES), jnp.bfloat16),
        in_specs=[pl.BlockSpec(memory_space=pltpu.HBM)] * 2,
        scratch_shapes=[
            pltpu.VMEM(queries.shape, queries.dtype),
            pltpu.VMEM(hits.shape, hits.dtype),
            pltpu.SemaphoreType.DMA((2,)),
        ],
        compiler_params=params(),
        cost_estimate=pl.CostEstimate(flops=PACK_COST, bytes_accessed=0, transcendentals=0),
        name="pack_queries",
    )(queries, hits)
    return out.reshape(devices, rows, LANES)


def rows_of(ref, g, slab):
    chips = ref.shape[0]
    pair = ref[:, (g // 2) * 2 * slab:(g // 2 + 1) * 2 * slab, :].astype(jnp.float32)
    at = (g % 2) * slab
    return pair[:, at:at + slab, :].reshape(chips * slab, LANES)


def one_hot(condition):
    return jnp.where(condition, 1.0, 0.0).astype(jnp.bfloat16)


def two_parts(x):
    high = x.astype(jnp.bfloat16)
    return high, (x - high.astype(jnp.float32)).astype(jnp.bfloat16)


def attend_body(own_rows, x_ref, *refs):
    *caches, out_ref, q_buf, y_buf = refs
    devices, msg_rows, _ = x_ref.shape
    slab = SLAB
    kv_heads = msg_rows // slab - 1
    group = slab // own_rows
    local_shards, positions, _ = caches[0].shape
    blocks = positions // KB
    cap = devices * own_rows // 2
    packed = group * cap
    both = devices * slab
    first_column = lax.rem(lax.axis_index("seq"), 2) * (kv_heads * HD)

    listed = x_ref[:, msg_rows - slab:, :].astype(jnp.float32).reshape(both, LANES)
    first = lax.axis_index("shard") * local_shards
    lane = lane_iota((both, LANES))
    slots = jnp.zeros((both, LANES), jnp.float32)
    for slot in range(local_shards):
        hit = jnp.sum(jnp.where(lane == first + slot, listed, 0.0), axis=1, keepdims=True)
        slots = jnp.where(lane == slot, hit, slots)

    def query_of(at):
        return lax.div(at, slab) * own_rows + lax.rem(at, own_rows)

    def head_of(at):
        return lax.div(lax.rem(at, slab), own_rows)

    row_query = query_of(lax.broadcasted_iota(jnp.int32, (both, both), 0))
    col_query = query_of(lax.broadcasted_iota(jnp.int32, (both, both), 1))
    earlier = one_hot(col_query < row_query)
    place = jnp.dot(earlier, slots.astype(jnp.bfloat16), preferred_element_type=jnp.float32)
    slots_t = jnp.transpose(slots)[:8]
    later = one_hot(row_query < col_query)
    place_t = jnp.dot(slots_t.astype(jnp.bfloat16), later, preferred_element_type=jnp.float32)

    def packed_key(at):
        return lax.div(at, cap), (lax.rem(at, cap) * group).astype(jnp.float32)

    pick_head, pick_place = packed_key(lax.broadcasted_iota(jnp.int32, (packed, both), 0))
    pick_from = head_of(lax.broadcasted_iota(jnp.int32, (packed, both), 1))
    back_head, back_place = packed_key(lax.broadcasted_iota(jnp.int32, (both, packed), 1))
    back_from = head_of(lax.broadcasted_iota(jnp.int32, (both, packed), 0))
    back = []
    queries = [rows_of(x_ref, g, slab) for g in range(kv_heads)]
    queries = jnp.concatenate(queries, axis=1).astype(jnp.bfloat16)
    for slot in range(local_shards):
        pick = one_hot(
            (pick_head == pick_from)
            & (pick_place == place_t[slot:slot + 1])
            & (slots_t[slot:slot + 1] > 0.0)
        )
        q_buf[slot] = jnp.dot(pick, queries, preferred_element_type=jnp.float32).astype(
            jnp.bfloat16
        )
        back.append(
            one_hot(
                (back_head == back_from)
                & (back_place == place[:, slot:slot + 1])
                & (slots[:, slot:slot + 1] > 0.0)
            )
        )

    ones = jnp.ones((KB, LANES), jnp.bfloat16)
    peak_of = []
    for slot in range(local_shards):
        tops = []
        for g in range(kv_heads):
            columns = pl.ds(pl.multiple_of(first_column + g * HD, HD), HD)
            query = q_buf[slot, :, g * HD:(g + 1) * HD]
            peaks, sums = [], []
            for block in range(2 * blocks):
                k_ref, v_ref = caches[2 * (block // blocks):2 * (block // blocks) + 2]
                at = slice(block % blocks * KB, (block % blocks + 1) * KB)
                scores = lax.dot_general(
                    k_ref[slot, at, columns], query, (((1,), (1,)), ((), ())),
                    preferred_element_type=jnp.float32,
                )
                peak = jnp.max(scores, axis=0, keepdims=True)
                weights = jnp.exp2((scores - peak) * TO_LOG2).astype(jnp.bfloat16)
                values = jnp.concatenate([v_ref[slot, at, columns], ones], axis=1)
                sums.append(
                    lax.dot_general(
                        weights, values, (((0,), (0,)), ((), ())),
                        preferred_element_type=jnp.float32,
                    )
                )
                peaks.append(peak * TO_LOG2)
            top = functools.reduce(jnp.maximum, peaks)
            factors = [jnp.exp2(peak - top) for peak in peaks]
            factors.append(jnp.zeros((8 - len(factors), packed), jnp.float32))
            factors = jnp.transpose(jnp.concatenate(factors, axis=0))
            total = sum(part * factors[:, i:i + 1] for i, part in enumerate(sums))
            high, low = two_parts(total)
            y_buf[slot, g] = jnp.concatenate([high, low], axis=0)
            tops.append(top)
        rest = jnp.concatenate(tops + [jnp.zeros_like(tops[0])] * (16 - kv_heads), axis=0)
        parts = []
        for _ in range(3):
            part = rest.astype(jnp.bfloat16)
            parts.append(part)
            rest = rest - part.astype(jnp.float32)
        peak = lax.dot_general(
            jnp.concatenate([back[slot]] * 3, axis=1), jnp.concatenate(parts, axis=1),
            (((1,), (1,)), ((), ())), preferred_element_type=jnp.float32,
        )
        peak_of.append(jnp.where(slots[:, slot:slot + 1] > 0.0, peak, NEG_FILL))

    top = functools.reduce(jnp.maximum, peak_of)
    factor_of = [jnp.where(peak > NEG_FILL, jnp.exp2(peak - top), 0.0) for peak in peak_of]
    twice = [jnp.concatenate([one] * 2, axis=1) for one in back]
    averages = []
    level = jnp.zeros((both, LANES), jnp.float32)
    for g in range(kv_heads):
        total = None
        for slot in range(local_shards):
            term = jnp.dot(twice[slot], y_buf[slot, g], preferred_element_type=jnp.float32)
            term = term * factor_of[slot][:, g:g + 1]
            total = term if total is None else total + term
        some = total[:, HD:] > 0.0
        safe = jnp.where(some, total[:, HD:], 1.0)
        averages.append((total[:, :HD] / safe).reshape(devices, slab, HD))
        weight = jnp.where(some, top[:, g:g + 1] + jnp.log2(safe), NEG_FILL)
        level = jnp.where(lane == g, weight, level)
    for pair in range(kv_heads // 2):
        out_ref[:, pair * 2 * slab:(pair + 1) * 2 * slab, :] = jnp.concatenate(
            averages[2 * pair:2 * pair + 2], axis=1
        ).astype(jnp.bfloat16)
    stats = jnp.zeros_like(level)
    for i in range(3):
        part = level.astype(jnp.bfloat16).astype(jnp.float32)
        level = level - part
        stats = stats + (pltpu.roll(part, PART * i, 1) if i else part)
    out_ref[:, msg_rows - slab:, :] = stats.reshape(devices, slab, LANES).astype(jnp.bfloat16)


def attend(message, caches, own_rows):
    devices, msg_rows, _ = message.shape
    kv_heads = msg_rows // SLAB - 1
    packed = SLAB * devices // 2
    keys = caches[0]
    local_shards = keys.shape[0]
    return pl.pallas_call(
        functools.partial(attend_body, own_rows),
        out_shape=jax.ShapeDtypeStruct(message.shape, jnp.bfloat16),
        scratch_shapes=[
            pltpu.VMEM((local_shards, packed, kv_heads * HD), jnp.bfloat16),
            pltpu.VMEM((local_shards, kv_heads, 2 * packed, 2 * LANES), jnp.bfloat16),
        ],
        compiler_params=params(),
        cost_estimate=pl.CostEstimate(
            flops=4 * packed * keys.size,
            bytes_accessed=4 * keys.size,
            transcendentals=packed * keys.size // HD,
        ),
        name="attend",
    )(message, *caches)


def finish_body(x_ref, out_ref):
    devices, msg_rows, _ = x_ref.shape
    own_rows, width = out_ref.shape
    slab = SLAB
    kv_heads = msg_rows // slab - 1
    stats = x_ref[:, msg_rows - slab:, :].astype(jnp.float32).reshape(devices * slab, LANES)
    level = stats
    for i in (1, 2):
        level = level + pltpu.roll(stats, LANES - PART * i, 1)
    level = level.reshape(devices // 2, 2, slab, LANES)
    top = jnp.max(level, axis=0, keepdims=True)
    factor = jnp.exp2(level - top)
    share = factor / jnp.sum(factor, axis=0, keepdims=True)
    pieces = []
    for core in range(2):
        for pair in range(kv_heads // 2):
            at = slice(pair * 2 * slab, (pair + 1) * 2 * slab)
            both = x_ref[:, at, :].astype(jnp.float32)
            both = both.reshape(devices // 2, 2, 2 * slab, LANES)[:, core]
            for i in range(2):
                g = 2 * pair + i
                part = both[:, i * slab:(i + 1) * slab, :] * share[:, core, :, g:g + 1]
                part = jnp.sum(part, axis=0)
                pieces += [
                    part[r * own_rows:(r + 1) * own_rows, :] for r in range(slab // own_rows)
                ]
    out_ref[...] = jnp.concatenate(pieces, axis=1).astype(jnp.bfloat16)


def finish(received, own_rows, width):
    return pl.pallas_call(
        finish_body,
        out_shape=jax.ShapeDtypeStruct((own_rows, width), jnp.bfloat16),
        compiler_params=params(),
        name="finish",
    )(received)


def shards(devices, queries, cached_keys, cached_values, shard_hits):
    axes = ("shard", "seq")
    siblings = [(i, i ^ 1) for i in range(devices)]
    caches = (
        cached_keys,
        cached_values,
        lax.ppermute(cached_keys, axes, siblings),
        lax.ppermute(cached_values, axes, siblings),
    )
    message = pack(queries, shard_hits, devices)
    received = lax.all_to_all(message, axes, 0, 0)
    partial = attend(received, caches, queries.shape[0])
    received = lax.all_to_all(partial, axes, 0, 0)
    return finish(received, *queries.shape)


def solution(mesh):
    both = P(("shard", "seq"), None)
    cache = P("shard", "seq", None)
    return jax.shard_map(
        functools.partial(shards, mesh.size),
        mesh=mesh,
        in_specs=(both, cache, cache, both),
        out_specs=both,
        check_vma=False,
    )
```

time: 47 us -> 43.2 us (0.919)
  waiting for transfers between devices: 3.45 us -> 0.01 us
  blocking collectives: 34.1 us -> 33.3 us
  local copies, waits for them, and re-layouts: 1.75 us -> 2.36 us
    ppermute x2, waiting for transfers between devices: 3.45 us -> 0.01 us  [the longest x1 0.01 us: shards(): lax.ppermute(cached_keys, axes, siblings)]
    all_to_all x2, blocking collectives: 34.1 us -> 33.3 us  [the longest x1 19.2 us: shards(): received = lax.all_to_all(message, axes, 0, 0)]
    unnamed x8, local copies, waits for them, and re-layouts: 1.75 us -> 2.36 us
    pallas_call x3 -> x2, Pallas kernels: 6.18 us -> 5.72 us  [the longest x1 5.67 us: attend(): pl.pallas_call(functools.partial(attend_body, own_rows), out_shape=jax.Sh...]
  transfers between devices with their start and end apart: 2 -> 2, of which waited for: 2 -> 0; matrix products, arithmetic and copies ran while one was open for 0% -> 0% of each run, Pallas kernels for 0% -> 0%
where the time goes in v3:
time: 43.2 us; the launch traced here: 42.9 us
  blocking collectives  33.3 us (77%)
  Pallas kernels  6.7 us (16%)
  local copies, waits for them, and re-layouts  2.36 us (5%)
  starting transfers between devices  0.53 us (1%)
    all_to_all x1, blocking collectives, shards(): received = lax.all_to_all(message, axes, 0, 0)  19.2 us
    all_to_all x1, blocking collectives, shards(): received = lax.all_to_all(partial, axes, 0, 0)  14.1 us
    pallas_call x1, Pallas kernels, attend(): pl.pallas_call(functools.partial(attend_body, own_rows), out_shape=jax.Sh...  5.67 us
    unnamed x8, local copies, waits for them, and re-layouts  2.36 us
    pallas_call x1, Pallas kernels, finish(): pl.pallas_call(finish_body, out_shape=jax.ShapeDtypeStruct((own_rows, wid...  0.97 us
  transfers between devices with their start and end apart: 2, of which 0 were waited for; matrix products, arithmetic and copies ran while one was open for 0% of the time, Pallas kernels for 0%

profile of v3, /device:TPU:0, one launch (start us, length us, event | category | flops | bytes accessed | tf_op | source)
XLA Modules:
  0.0 42.9 jit_solution(9275643245296322323)
XLA Ops:
  0.0 0.0 copy-start
  0.0 0.0 copy-start.1
  0.0 0.5 %collective-permute-start = (bf16[2,1024,1024]{2,1,0:T(8,128)(2,1)}, bf16[2,1024,1024]{2,1,0:T(8,128)(2,1)S(1)}, u32[]{:S(2)}, u32[]{:S(2)}) collective-permute-start(bf16[2,1024,1024]{2,1,0:T(8,128)(2,1)} %refs_0_.1), channel_id=1, source_target_pairs={{0,1},{1,0},{2,3},{3,2},{4,5},{5,4},{6,7},{7,6},{8,9},{9,8},{10,11... | collective-permute-start | bytes 12582920 | tf_op jit(solution)/shard_map/ppermute | solution.py:295
  0.5 0.1 collective-permute-start.1
  0.5 0.0 copy-start.2
  0.5 1.0 %copy-done.2 = bf16[2,4096]{1,0:T(2,128)(2,1)S(1)} copy-done((bf16[2,4096]{1,0:T(2,128)(2,1)S(1)}, bf16[2,4096]{1,0:T(2,128)(2,1)}, u32[]{:S(2)}) %copy-start.2) | copy-done | bytes 16408
  1.5 0.0 copy-start.3
  1.5 1.4 %copy-done.3 = s32[2,8]{1,0:T(2,128)S(1)} copy-done((s32[2,8]{1,0:T(2,128)S(1)}, s32[2,8]{1,0:T(2,128)}, u32[]{:S(2)}) %copy-start.3) | copy-done | bytes 88
  2.9 0.1 pack_queries.1
  3.0 19.2 %all_to_all.10.x_ref = bf16[32,40,128]{2,1,0:T(8,128)(2,1)S(1)} all-to-all(bf16[32,40,128]{2,1,0:T(8,128)(2,1)S(1)} %bitcast.1), channel_id=1, replica_groups=mesh['shard'=4,'seq'=8] {'shard','seq'}, dimensions={0} | all-to-all | bytes 655360 | tf_op jit(solution)/shard_map/all_to_all | solution.py:299
  22.2 0.0 collective-permute-done.refs_2_
  22.2 0.0 collective-permute-done.1.refs_3_
  22.2 0.0 copy-done
  22.2 0.0 copy-done.1
  22.2 5.7 %attend.1 = bf16[32,40,128]{2,1,0:T(8,128)(2,1)S(1)} custom-call(bf16[32,40,128]{2,1,0:T(8,128)(2,1)S(1)} %all_to_all.10.x_ref, bf16[2,1024,1024]{2,1,0:T(8,128)(2,1)S(1)} %copy-done, bf16[2,1024,1024]{2,1,0:T(8,128)(2,1)S(1)} %copy-done.1, bf16[2,1024,1024]{2,1,0:T(8,128)(2,1)S(1)} %collective-permute-done.refs_2_, ...), custom_call_target="tpu_custom_call" | custom-call | flops 1073741824 | bytes 8388608 | tf_op jit(solution)/shard_map/attend/pallas_call | solution.py:234
  27.9 14.1 %all_to_all.11.x_ref = bf16[32,40,128]{2,1,0:T(8,128)(2,1)S(1)} all-to-all(bf16[32,40,128]{2,1,0:T(8,128)(2,1)S(1)} %attend.1), channel_id=1, replica_groups=mesh['shard'=4,'seq'=8] {'shard','seq'}, dimensions={0} | all-to-all | bytes 655360 | tf_op jit(solution)/shard_map/all_to_all | solution.py:301
  42.0 1.0 %finish.1 = bf16[2,4096]{1,0:T(2,128)(2,1)} custom-call(bf16[32,40,128]{2,1,0:T(8,128)(2,1)S(1)} %all_to_all.11.x_ref), custom_call_target="tpu_custom_call" | custom-call | tf_op jit(solution)/shard_map/finish/pallas_call | solution.py:281
Async XLA Ops:
  0.0 22.2 %copy-start = (bf16[2,1024,1024]{2,1,0:T(8,128)(2,1)S(1)}, bf16[2,1024,1024]{2,1,0:T(8,128)(2,1)}, u32[]{:S(2)}) copy-start(bf16[2,1024,1024]{2,1,0:T(8,128)(2,1)} %refs_0_.1) | copy-start | bytes 12582916
  0.0 22.2 %copy-start.1 = (bf16[2,1024,1024]{2,1,0:T(8,128)(2,1)S(1)}, bf16[2,1024,1024]{2,1,0:T(8,128)(2,1)}, u32[]{:S(2)}) copy-start(bf16[2,1024,1024]{2,1,0:T(8,128)(2,1)} %refs_1_.1) | copy-start | bytes 12582916
  0.0 22.2 %collective-permute-start = (bf16[2,1024,1024]{2,1,0:T(8,128)(2,1)}, bf16[2,1024,1024]{2,1,0:T(8,128)(2,1)S(1)}, u32[]{:S(2)}, u32[]{:S(2)}) collective-permute-start(bf16[2,1024,1024]{2,1,0:T(8,128)(2,1)} %refs_0_.1), channel_id=1, source_target_pairs={{0,1},{1,0},{2,3},{3,2},{4,5},{5,4},{6,7},{7,6},{8,9},{9,8},{10,11... | collective-permute-start | bytes 12582920 | tf_op jit(solution)/shard_map/ppermute | solution.py:295
  0.5 21.7 %collective-permute-start.1 = (bf16[2,1024,1024]{2,1,0:T(8,128)(2,1)}, bf16[2,1024,1024]{2,1,0:T(8,128)(2,1)S(1)}, u32[]{:S(2)}, u32[]{:S(2)}) collective-permute-start(bf16[2,1024,1024]{2,1,0:T(8,128)(2,1)} %refs_1_.1), channel_id=1, source_target_pairs={{0,1},{1,0},{2,3},{3,2},{4,5},{5,4},{6,7},{7,6},{8,9},{9,8},{10,11... | collective-permute-start | bytes 12582920 | tf_op jit(solution)/shard_map/ppermute | solution.py:296
  0.5 1.0 %copy-start.2 = (bf16[2,4096]{1,0:T(2,128)(2,1)S(1)}, bf16[2,4096]{1,0:T(2,128)(2,1)}, u32[]{:S(2)}) copy-start(bf16[2,4096]{1,0:T(2,128)(2,1)} %queries_hbm.1) | copy-start | bytes 49156
  1.5 1.4 %copy-start.3 = (s32[2,8]{1,0:T(2,128)S(1)}, s32[2,8]{1,0:T(2,128)}, u32[]{:S(2)}) copy-start(s32[2,8]{1,0:T(2,128)} %hits_hbm.1) | copy-start | bytes 196

commit v4 on v3

v4 whole, which is shorter than its diff:
```python
import functools
import math

import jax
import jax.numpy as jnp
from jax import lax
from jax.experimental import pallas as pl
from jax.experimental.pallas import tpu as pltpu
from jax.sharding import PartitionSpec as P

HD = 128
KB = 512
LANES = 128
NEG_FILL = -1e30
TO_LOG2 = math.log2(math.e) / math.sqrt(HD)
PACK_COST = 20_000_000_000
VMEM_LIMIT = 24 * 1024 * 1024
PART = 32
SUBLANES = 8


def params():
    return pltpu.CompilerParams(vmem_limit_bytes=VMEM_LIMIT)


def lane_iota(shape):
    return lax.broadcasted_iota(jnp.int32, shape, len(shape) - 1)


def one_hot(condition):
    return jnp.where(condition, 1.0, 0.0).astype(jnp.bfloat16)


def dot(a, b):
    return jnp.dot(a, b, preferred_element_type=jnp.float32)


def parts_of(x, count):
    parts = []
    for _ in range(count):
        part = x.astype(jnp.bfloat16)
        parts.append(part)
        x = x - part.astype(jnp.float32)
    return parts


def pack_body(x_ref, out_ref):
    half = (x_ref.shape[1] - LANES) // 2
    x = x_ref[...]
    for core in range(2):
        message = jnp.concatenate([x[:, core * half:(core + 1) * half], x[:, 2 * half:]], axis=1)
        out_ref[:, core] = jnp.broadcast_to(message[None], (out_ref.shape[0],) + message.shape)


def pack(queries, hits, devices):
    own_rows, width = queries.shape
    hits = jnp.pad(hits.astype(jnp.bfloat16), ((0, 0), (0, LANES - hits.shape[1])))
    shape = (devices // 2, 2, own_rows, width // 2 + LANES)
    out = pl.pallas_call(
        pack_body,
        out_shape=jax.ShapeDtypeStruct(shape, jnp.bfloat16),
        compiler_params=params(),
        cost_estimate=pl.CostEstimate(flops=PACK_COST, bytes_accessed=0, transcendentals=0),
        name="pack_queries",
    )(jnp.concatenate([queries, hits], axis=1))
    return out.reshape(devices, own_rows, width // 2 + LANES)


def attend_body(x_ref, *refs):
    *caches, out_ref, q_buf, y_buf = refs
    devices, own_rows, message = x_ref.shape
    width = message - LANES
    heads = width // HD
    local_shards, positions, cache_width = caches[0].shape
    kv_heads = cache_width // HD // 2
    group = heads // kv_heads
    blocks = positions // KB
    rows = devices * own_rows
    cap = rows // 2
    packed = group * cap
    first_column = lax.rem(lax.axis_index("seq"), 2) * (kv_heads * HD)

    x = x_ref[...].reshape(rows, message)
    listed = x[:, width:].astype(jnp.float32)
    first = lax.axis_index("shard") * local_shards
    lane = lane_iota((rows, LANES))
    slots = jnp.zeros((rows, LANES), jnp.float32)
    for slot in range(local_shards):
        hit = jnp.sum(jnp.where(lane == first + slot, listed, 0.0), axis=1, keepdims=True)
        slots = jnp.where(lane == slot, hit, slots)
    hits = [slots[:, slot:slot + 1] > 0.0 for slot in range(local_shards)]
    row = lax.broadcasted_iota(jnp.int32, (rows, rows), 0)
    column = lax.broadcasted_iota(jnp.int32, (rows, rows), 1)
    place = dot(one_hot(column < row), slots.astype(jnp.bfloat16))
    slots_t = jnp.transpose(slots)[:SUBLANES]
    place_t = dot(slots_t.astype(jnp.bfloat16), one_hot(row < column))

    pick_at = lax.broadcasted_iota(jnp.int32, (cap, rows), 0).astype(jnp.float32)
    picks, backs = [], []
    for slot in range(local_shards):
        picks.append(
            one_hot((pick_at == place_t[slot:slot + 1]) & (slots_t[slot:slot + 1] > 0.0))
        )
        q_buf[slot] = dot(picks[slot], x[:, :width]).astype(jnp.bfloat16)
        back_at = lax.rem(lane_iota((rows, 3 * cap)), cap).astype(jnp.float32)
        backs.append(one_hot((back_at == place[:, slot:slot + 1]) & hits[slot]))

    ones = jnp.ones((KB, LANES), jnp.bfloat16)
    cap_lane = lane_iota((cap, LANES))
    levels = []
    for slot in range(local_shards):
        level = jnp.zeros((cap, LANES), jnp.float32)
        for g in range(kv_heads):
            columns = pl.ds(pl.multiple_of(first_column + g * HD, HD), HD)
            group_heads = [g * group + r for r in range(group)]
            query = jnp.concatenate(
                [q_buf[slot, :, h * HD:(h + 1) * HD] for h in group_heads], axis=0
            )
            peaks, sums = [], []
            for block in range(2 * blocks):
                k_ref, v_ref = caches[2 * (block // blocks):2 * (block // blocks) + 2]
                at = slice(block % blocks * KB, (block % blocks + 1) * KB)
                scores = lax.dot_general(
                    k_ref[slot, at, columns], query, (((1,), (1,)), ((), ())),
                    preferred_element_type=jnp.float32,
                )
                peak = jnp.max(scores, axis=0, keepdims=True)
                weights = jnp.exp2((scores - peak) * TO_LOG2).astype(jnp.bfloat16)
                values = jnp.concatenate([v_ref[slot, at, columns], ones], axis=1)
                sums.append(
                    lax.dot_general(
                        weights, values, (((0,), (0,)), ((), ())),
                        preferred_element_type=jnp.float32,
                    )
                )
                peaks.append(peak * TO_LOG2)
            top = functools.reduce(jnp.maximum, peaks)
            factors = [top] + [jnp.exp2(peak - top) for peak in peaks]
            factors.append(jnp.zeros((SUBLANES - len(factors), packed), jnp.float32))
            factors = jnp.transpose(jnp.concatenate(factors, axis=0))
            total = sum(part * factors[:, i + 1:i + 2] for i, part in enumerate(sums))
            average = total[:, :HD] / total[:, HD:]
            log_total = factors[:, :1] + jnp.log2(total[:, HD:])
            for r, h in enumerate(group_heads):
                at = slice(r * cap, (r + 1) * cap)
                y_buf[slot, :, h * HD:(h + 1) * HD] = average[at]
                level = jnp.where(cap_lane == h, log_total[at], level)
        levels.append(level)

    level_of = []
    for slot in range(local_shards):
        level = dot(backs[slot], jnp.concatenate(parts_of(levels[slot], 3), axis=0))
        level_of.append(jnp.where(hits[slot], level, NEG_FILL))
    top = functools.reduce(jnp.maximum, level_of)
    shares = [
        jnp.where(hit, jnp.exp2(level - top), 0.0) for hit, level in zip(hits, level_of)
    ]
    share_sum = sum(shares)
    some = share_sum > 0.0
    share_sum = jnp.where(some, share_sum, 1.0)
    merged_level = jnp.where(some, top + jnp.log2(share_sum), NEG_FILL)
    scaled = []
    for slot in range(local_shards):
        share = sum(dot(picks[slot], part) for part in parts_of(shares[slot] / share_sum, 2))
        columns = [
            y_buf[slot, :, h * HD:(h + 1) * HD] * share[:, h:h + 1] for h in range(heads)
        ]
        scaled += parts_of(jnp.concatenate(columns, axis=1), 2)
    back_at = lane_iota((rows, 2 * local_shards * cap))
    back_place = lax.rem(back_at, cap).astype(jnp.float32)
    back_slot = lax.div(back_at, 2 * cap)
    back = functools.reduce(
        jnp.logical_or,
        [
            (back_slot == slot) & (back_place == place[:, slot:slot + 1]) & hits[slot]
            for slot in range(local_shards)
        ],
    )
    merged = dot(one_hot(back), jnp.concatenate(scaled, axis=0))
    stats = jnp.zeros((rows, LANES), jnp.float32)
    level_parts = parts_of(jnp.where(lane < heads, merged_level, 0.0), 3)
    for i, part in enumerate(level_parts):
        part = part.astype(jnp.float32)
        stats = stats + (pltpu.roll(part, PART * i, 1) if i else part)
    out = jnp.concatenate([merged, stats], axis=1).astype(jnp.bfloat16)
    out_ref[...] = out.reshape(out_ref.shape)


def attend(message, caches):
    devices, own_rows, columns = message.shape
    keys = caches[0]
    local_shards = keys.shape[0]
    cap = devices * own_rows // 2
    width = columns - LANES
    scores = 2 * cap * width // HD * local_shards * keys.shape[1]
    return pl.pallas_call(
        attend_body,
        out_shape=jax.ShapeDtypeStruct(message.shape, jnp.bfloat16),
        scratch_shapes=[
            pltpu.VMEM((local_shards, cap, width), jnp.bfloat16),
            pltpu.VMEM((local_shards, cap, width), jnp.float32),
        ],
        compiler_params=params(),
        cost_estimate=pl.CostEstimate(
            flops=4 * scores * HD, bytes_accessed=4 * keys.size, transcendentals=scores
        ),
        name="attend",
    )(message, *caches)


def finish_body(x_ref, out_ref):
    devices, own_rows, message = x_ref.shape
    width = message - LANES
    rows = devices * own_rows
    period = 2 * own_rows

    def over_chips(x, combine):
        x = functools.reduce(combine, [x[i] for i in range(x.shape[0])])
        shift = period
        while shift < SUBLANES:
            x = combine(x, pltpu.roll(x, shift, 0))
            shift *= 2
        return x

    def tiles(x):
        return x.reshape(rows // SUBLANES, SUBLANES, x.shape[1])

    x = x_ref[...].reshape(rows, message).astype(jnp.float32)
    stats = x[:, width:]
    level = stats
    for i in (1, 2):
        level = level + pltpu.roll(stats, LANES - PART * i, 1)
    level = tiles(level)
    factor = jnp.exp2(level - over_chips(level, jnp.maximum)[None])
    share = factor / over_chips(factor, jnp.add)[None]
    pieces = [
        over_chips(tiles(x[:, h * HD:(h + 1) * HD]) * share[:, :, h:h + 1], jnp.add)
        for h in range(width // HD)
    ]
    merged = jnp.concatenate(pieces, axis=1)
    out_ref[...] = jnp.concatenate(
        [merged[core * own_rows:(core + 1) * own_rows] for core in range(2)], axis=1
    ).astype(jnp.bfloat16)


def finish(received, own_rows, width):
    return pl.pallas_call(
        finish_body,
        out_shape=jax.ShapeDtypeStruct((own_rows, width), jnp.bfloat16),
        compiler_params=params(),
        name="finish",
    )(received)


def shards(devices, queries, cached_keys, cached_values, shard_hits):
    axes = ("shard", "seq")
    siblings = [(i, i ^ 1) for i in range(devices)]
    caches = (
        cached_keys,
        cached_values,
        lax.ppermute(cached_keys, axes, siblings),
        lax.ppermute(cached_values, axes, siblings),
    )
    message = pack(queries, shard_hits, devices)
    received = lax.all_to_all(message, axes, 0, 0)
    partial = attend(received, caches)
    received = lax.all_to_all(partial, axes, 0, 0)
    return finish(received, *queries.shape)


def solution(mesh):
    both = P(("shard", "seq"), None)
    cache = P("shard", "seq", None)
    return jax.shard_map(
        functools.partial(shards, mesh.size),
        mesh=mesh,
        in_specs=(both, cache, cache, both),
        out_specs=both,
        check_vma=False,
    )
```

time: 43.2 us -> 40.6 us (0.940)
  local copies, waits for them, and re-layouts: 2.36 us -> 0.01 us
  blocking collectives: 33.3 us -> 31.3 us
  other arithmetic: 0 us -> 1.42 us
    unnamed x8 -> x4, local copies, waits for them, and re-layouts: 2.36 us -> 0.01 us
    all_to_all x1, blocking collectives: 14.1 us -> 13.1 us  [shards(): received = lax.all_to_all(partial, axes, 0, 0)]
    all_to_all x1, blocking collectives: 19.2 us -> 18.2 us  [shards(): received = lax.all_to_all(message, axes, 0, 0)]
    concatenate x0 -> x1, other arithmetic: none -> 0.73 us  [pack(): jnp.concatenate([queries, hits], axis=1)]
    convert_element_type x0 -> x1, other arithmetic: none -> 0.68 us  [pack(): hits.astype(jnp.bfloat16)]
    pallas_call x1, Pallas kernels: 0.97 us -> 1.42 us  [finish(): pl.pallas_call(finish_body, out_shape=jax.ShapeDtypeStruct((own_rows, wid...]
  transfers between devices with their start and end apart: 2 -> 2, of which waited for: 0 -> 0; matrix products, arithmetic and copies ran while one was open for 0% -> 4% of each run, Pallas kernels for 0% -> 0%
where the time goes in v4:
time: 40.6 us; the launch traced here: 40.3 us
  blocking collectives  31.3 us (77%)
  Pallas kernels  7.08 us (17%)
  other arithmetic  1.42 us (3%)
  starting transfers between devices  0.51 us (1%)
    all_to_all x1, blocking collectives, shards(): received = lax.all_to_all(message, axes, 0, 0)  18.2 us
    all_to_all x1, blocking collectives, shards(): received = lax.all_to_all(partial, axes, 0, 0)  13.1 us
    pallas_call x1, Pallas kernels, attend(): pl.pallas_call(attend_body, out_shape=jax.ShapeDtypeStruct(message.shape,...  5.62 us
    pallas_call x1, Pallas kernels, finish(): pl.pallas_call(finish_body, out_shape=jax.ShapeDtypeStruct((own_rows, wid...  1.42 us
  transfers between devices with their start and end apart: 2, of which 0 were waited for; matrix products, arithmetic and copies ran while one was open for 4% of the time, Pallas kernels for 0%

profile of v4, /device:TPU:0, one launch (start us, length us, event | category | flops | bytes accessed | tf_op | source)
XLA Modules:
  0.0 40.3 jit_solution(1470415209360466723)
XLA Ops:
  0.0 0.5 %collective-permute-start = (bf16[2,1024,1024]{2,1,0:T(8,128)(2,1)}, bf16[2,1024,1024]{2,1,0:T(8,128)(2,1)S(1)}, u32[]{:S(2)}, u32[]{:S(2)}) collective-permute-start(bf16[2,1024,1024]{2,1,0:T(8,128)(2,1)} %refs_0_.1), channel_id=1, source_target_pairs={{0,1},{1,0},{2,3},{3,2},{4,5},{5,4},{6,7},{7,6},{8,9},{9,8},{10,11... | collective-permute-start | bytes 12582920 | tf_op jit(solution)/shard_map/ppermute | solution.py:261
  0.5 0.1 collective-permute-start.1
  0.5 0.7 %convert_element_type.5 = bf16[2,8]{1,0:T(2,128)(2,1)S(1)} convert(s32[2,8]{1,0:T(2,128)} %param.7) | non-fusion elementwise | flops 16 | bytes 96 | tf_op jit(solution)/shard_map/convert_element_type | solution.py:57
  1.2 0.7 %fusion.x_ref = bf16[2,4224]{1,0:T(2,128)(2,1)S(1)} fusion(bf16[2,8]{1,0:T(2,128)(2,1)S(1)} %convert_element_type.5, bf16[2,4096]{1,0:T(2,128)(2,1)} %param.4), kind=kLoop, calls=%fused_computation.1 | loop fusion | flops 50688 | bytes 33312 | tf_op jit(solution)/shard_map/concatenate | solution.py:65
  1.9 0.0 copy-start
  1.9 0.0 copy-start.1
  2.0 18.2 %all_to_all.10.x_ref = bf16[32,2,2176]{2,1,0:T(2,128)(2,1)S(1)} all-to-all(bf16[32,2,2176]{2,1,0:T(2,128)(2,1)S(1)} %bitcast.1), channel_id=1, replica_groups=mesh['shard'=4,'seq'=8] {'shard','seq'}, dimensions={0} | all-to-all | bytes 557056 | tf_op jit(solution)/shard_map/all_to_all | solution.py:265
  20.2 0.0 collective-permute-done.refs_2_
  20.2 0.0 collective-permute-done.1.refs_3_
  20.2 0.0 copy-done
  20.2 0.0 copy-done.1
  20.2 5.6 %attend.1 = bf16[32,2,2176]{2,1,0:T(2,128)(2,1)S(1)} custom-call(bf16[32,2,2176]{2,1,0:T(2,128)(2,1)S(1)} %all_to_all.10.x_ref, bf16[2,1024,1024]{2,1,0:T(8,128)(2,1)S(1)} %copy-done, bf16[2,1024,1024]{2,1,0:T(8,128)(2,1)S(1)} %copy-done.1, bf16[2,1024,1024]{2,1,0:T(8,128)(2,1)S(1)} %collective-permute-done.refs_2_, ...), custom_call_target="tpu_custom_call" | custom-call | flops 1073741824 | bytes 8388608 | tf_op jit(solution)/shard_map/attend/pallas_call | solution.py:196
  25.8 13.1 %all_to_all.11.x_ref = bf16[32,2,2176]{2,1,0:T(2,128)(2,1)S(1)} all-to-all(bf16[32,2,2176]{2,1,0:T(2,128)(2,1)S(1)} %attend.1), channel_id=1, replica_groups=mesh['shard'=4,'seq'=8] {'shard','seq'}, dimensions={0} | all-to-all | bytes 557056 | tf_op jit(solution)/shard_map/all_to_all | solution.py:267
  38.9 1.4 %finish.1 = bf16[2,4096]{1,0:T(2,128)(2,1)} custom-call(bf16[32,2,2176]{2,1,0:T(2,128)(2,1)S(1)} %all_to_all.11.x_ref), custom_call_target="tpu_custom_call" | custom-call | tf_op jit(solution)/shard_map/finish/pallas_call | solution.py:247
  (1 shorter events, 0.0 us)
Async XLA Ops:
  0.0 20.2 %collective-permute-start = (bf16[2,1024,1024]{2,1,0:T(8,128)(2,1)}, bf16[2,1024,1024]{2,1,0:T(8,128)(2,1)S(1)}, u32[]{:S(2)}, u32[]{:S(2)}) collective-permute-start(bf16[2,1024,1024]{2,1,0:T(8,128)(2,1)} %refs_0_.1), channel_id=1, source_target_pairs={{0,1},{1,0},{2,3},{3,2},{4,5},{5,4},{6,7},{7,6},{8,9},{9,8},{10,11... | collective-permute-start | bytes 12582920 | tf_op jit(solution)/shard_map/ppermute | solution.py:261
  0.5 19.7 %collective-permute-start.1 = (bf16[2,1024,1024]{2,1,0:T(8,128)(2,1)}, bf16[2,1024,1024]{2,1,0:T(8,128)(2,1)S(1)}, u32[]{:S(2)}, u32[]{:S(2)}) collective-permute-start(bf16[2,1024,1024]{2,1,0:T(8,128)(2,1)} %refs_1_.1), channel_id=1, source_target_pairs={{0,1},{1,0},{2,3},{3,2},{4,5},{5,4},{6,7},{7,6},{8,9},{9,8},{10,11... | collective-permute-start | bytes 12582920 | tf_op jit(solution)/shard_map/ppermute | solution.py:262
  1.9 18.3 %copy-start = (bf16[2,1024,1024]{2,1,0:T(8,128)(2,1)S(1)}, bf16[2,1024,1024]{2,1,0:T(8,128)(2,1)}, u32[]{:S(2)}) copy-start(bf16[2,1024,1024]{2,1,0:T(8,128)(2,1)} %refs_0_.1) | copy-start | bytes 12582916
  1.9 18.3 %copy-start.1 = (bf16[2,1024,1024]{2,1,0:T(8,128)(2,1)S(1)}, bf16[2,1024,1024]{2,1,0:T(8,128)(2,1)}, u32[]{:S(2)}) copy-start(bf16[2,1024,1024]{2,1,0:T(8,128)(2,1)} %refs_1_.1) | copy-start | bytes 12582916

commit v5 on v4

--- a/solution.py
+++ b/solution.py
@@ -54,7 +54,8 @@
 
 def pack(queries, hits, devices):
     own_rows, width = queries.shape
-    hits = jnp.pad(hits.astype(jnp.bfloat16), ((0, 0), (0, LANES - hits.shape[1])))
+    listed = jnp.pad(hits, ((0, 0), (width, LANES - hits.shape[1]))) > 0
+    joined = jnp.where(listed, 1.0, jnp.pad(queries, ((0, 0), (0, LANES)))).astype(queries.dtype)
     shape = (devices // 2, 2, own_rows, width // 2 + LANES)
     out = pl.pallas_call(
         pack_body,
@@ -62,7 +63,7 @@
         compiler_params=params(),
         cost_estimate=pl.CostEstimate(flops=PACK_COST, bytes_accessed=0, transcendentals=0),
         name="pack_queries",
-    )(jnp.concatenate([queries, hits], axis=1))
+    )(joined)
     return out.reshape(devices, own_rows, width // 2 + LANES)
 
 
@@ -105,13 +106,15 @@
         back_at = lax.rem(lane_iota((rows, 3 * cap)), cap).astype(jnp.float32)
         backs.append(one_hot((back_at == place[:, slot:slot + 1]) & hits[slot]))
 
+    mine = pl.ds(pl.multiple_of(first_column, HD), kv_heads * HD)
+    caches = [ref.at[:, :, mine] for ref in caches]
     ones = jnp.ones((KB, LANES), jnp.bfloat16)
     cap_lane = lane_iota((cap, LANES))
     levels = []
     for slot in range(local_shards):
         level = jnp.zeros((cap, LANES), jnp.float32)
         for g in range(kv_heads):
-            columns = pl.ds(pl.multiple_of(first_column + g * HD, HD), HD)
+            columns = slice(g * HD, (g + 1) * HD)
             group_heads = [g * group + r for r in range(group)]
             query = jnp.concatenate(
                 [q_buf[slot, :, h * HD:(h + 1) * HD] for h in group_heads], axis=0
@@ -211,6 +214,7 @@
 def finish_body(x_ref, out_ref):
     devices, own_rows, message = x_ref.shape
     width = message - LANES
+    heads = width // HD
     rows = devices * own_rows
     period = 2 * own_rows
 
@@ -222,21 +226,27 @@
             shift *= 2
         return x
 
-    def tiles(x):
-        return x.reshape(rows // SUBLANES, SUBLANES, x.shape[1])
-
-    x = x_ref[...].reshape(rows, message).astype(jnp.float32)
-    stats = x[:, width:]
+    x = x_ref[...].reshape(rows, message)
+    stats = x[:, width:].astype(jnp.float32)
     level = stats
     for i in (1, 2):
         level = level + pltpu.roll(stats, LANES - PART * i, 1)
-    level = tiles(level)
+    level = level.reshape(rows // SUBLANES, SUBLANES, LANES)
     factor = jnp.exp2(level - over_chips(level, jnp.maximum)[None])
     share = factor / over_chips(factor, jnp.add)[None]
-    pieces = [
-        over_chips(tiles(x[:, h * HD:(h + 1) * HD]) * share[:, :, h:h + 1], jnp.add)
-        for h in range(width // HD)
-    ]
+    share = jnp.transpose(share.reshape(rows, LANES))[:heads]
+    high, low = parts_of(share, 2)
+    target = lax.broadcasted_iota(jnp.int32, (SUBLANES, rows), 0)
+    source = lax.broadcasted_iota(jnp.int32, (SUBLANES, rows), 1)
+    mine = target == lax.rem(source, period)
+    high, low = high.astype(jnp.float32), low.astype(jnp.float32)
+    pieces = []
+    for h in range(heads):
+        weights = jnp.concatenate(
+            [jnp.where(mine, part[h:h + 1], 0.0) for part in (high, low)], axis=0
+        ).astype(jnp.bfloat16)
+        both = dot(weights, x[:, h * HD:(h + 1) * HD])
+        pieces.append(both[:SUBLANES] + both[SUBLANES:])
     merged = jnp.concatenate(pieces, axis=1)
     out_ref[...] = jnp.concatenate(
         [merged[core * own_rows:(core + 1) * own_rows] for core in range(2)], axis=1

time: 40.6 us -> 39.1 us (0.963)
  Pallas kernels: 7.08 us -> 6.25 us
  other arithmetic: 1.42 us -> 0.75 us
    select_n x0 -> x1, other arithmetic: none -> 0.75 us  [pack(): jnp.where(listed, 1.0, jnp.pad(queries, ((0, 0), (0, LANES))))]
    concatenate x1 -> x0, other arithmetic: 0.73 us -> none  [pack(): jnp.concatenate([queries, hits], axis=1)]
    convert_element_type x1 -> x0, other arithmetic: 0.68 us -> none  [pack(): hits.astype(jnp.bfloat16)]
    pallas_call x1, Pallas kernels: 5.62 us -> 5.2 us  [attend(): pl.pallas_call(attend_body, out_shape=jax.ShapeDtypeStruct(message.shape,...]
  transfers between devices with their start and end apart: 2 -> 2, of which waited for: 0 -> 0; matrix products, arithmetic and copies ran while one was open for 4% -> 2% of each run, Pallas kernels for 0% -> 0%
where the time goes in v5:
time: 39.1 us; the launch traced here: 38.8 us
  blocking collectives  31.3 us (80%)
  Pallas kernels  6.25 us (16%)
  other arithmetic  0.75 us (2%)
  starting transfers between devices  0.51 us (1%)
    all_to_all x1, blocking collectives, shards(): received = lax.all_to_all(message, axes, 0, 0)  18.2 us
    all_to_all x1, blocking collectives, shards(): received = lax.all_to_all(partial, axes, 0, 0)  13.1 us
    pallas_call x1, Pallas kernels, attend(): pl.pallas_call(attend_body, out_shape=jax.ShapeDtypeStruct(message.shape,...  5.2 us
    pallas_call x1, Pallas kernels, finish(): pl.pallas_call(finish_body, out_shape=jax.ShapeDtypeStruct((own_rows, wid...  1.02 us
  transfers between devices with their start and end apart: 2, of which 0 were waited for; matrix products, arithmetic and copies ran while one was open for 2% of the time, Pallas kernels for 0%

profile of v5, /device:TPU:0, one launch (start us, length us, event | category | flops | bytes accessed | tf_op | source)
XLA Modules:
  0.0 38.8 jit_solution(13863696835501806918)
XLA Ops:
  0.0 0.5 %collective-permute-start = (bf16[2,1024,1024]{2,1,0:T(8,128)(2,1)}, bf16[2,1024,1024]{2,1,0:T(8,128)(2,1)S(1)}, u32[]{:S(2)}, u32[]{:S(2)}) collective-permute-start(bf16[2,1024,1024]{2,1,0:T(8,128)(2,1)} %refs_0_.1), channel_id=1, source_target_pairs={{0,1},{1,0},{2,3},{3,2},{4,5},{5,4},{6,7},{7,6},{8,9},{9,8},{10,11... | collective-permute-start | bytes 12582920 | tf_op jit(solution)/shard_map/ppermute | solution.py:271
  0.5 0.1 collective-permute-start.1
  0.5 0.8 %compare_select_fusion.x_ref = bf16[2,4224]{1,0:T(2,128)(2,1)S(1)} fusion(s32[2,8]{1,0:T(2,128)} %param.7, bf16[2,4096]{1,0:T(2,128)(2,1)} %param.4), kind=kLoop, calls=%fused_computation | loop fusion | flops 16896 | bytes 33344 | tf_op jit(solution)/shard_map/jit(_where)/select_n | solution.py:58
  1.3 0.0 copy-start
  1.3 0.0 copy-start.1
  1.3 18.2 %all_to_all.10.x_ref = bf16[32,2,2176]{2,1,0:T(2,128)(2,1)S(1)} all-to-all(bf16[32,2,2176]{2,1,0:T(2,128)(2,1)S(1)} %bitcast.1), channel_id=1, replica_groups=mesh['shard'=4,'seq'=8] {'shard','seq'}, dimensions={0} | all-to-all | bytes 557056 | tf_op jit(solution)/shard_map/all_to_all | solution.py:275
  19.5 0.0 collective-permute-done.refs_2_
  19.5 0.0 collective-permute-done.1.refs_3_
  19.5 0.0 copy-done
  19.5 0.0 copy-done.1
  19.5 5.2 %attend.1 = bf16[32,2,2176]{2,1,0:T(2,128)(2,1)S(1)} custom-call(bf16[32,2,2176]{2,1,0:T(2,128)(2,1)S(1)} %all_to_all.10.x_ref, bf16[2,1024,1024]{2,1,0:T(8,128)(2,1)S(1)} %copy-done, bf16[2,1024,1024]{2,1,0:T(8,128)(2,1)S(1)} %copy-done.1, bf16[2,1024,1024]{2,1,0:T(8,128)(2,1)S(1)} %collective-permute-done.refs_2_, ...), custom_call_target="tpu_custom_call" | custom-call | flops 1073741824 | bytes 8388608 | tf_op jit(solution)/shard_map/attend/pallas_call | solution.py:199
  24.7 13.1 %all_to_all.11.x_ref = bf16[32,2,2176]{2,1,0:T(2,128)(2,1)S(1)} all-to-all(bf16[32,2,2176]{2,1,0:T(2,128)(2,1)S(1)} %attend.1), channel_id=1, replica_groups=mesh['shard'=4,'seq'=8] {'shard','seq'}, dimensions={0} | all-to-all | bytes 557056 | tf_op jit(solution)/shard_map/all_to_all | solution.py:277
  37.8 1.0 %finish.1 = bf16[2,4096]{1,0:T(2,128)(2,1)} custom-call(bf16[32,2,2176]{2,1,0:T(2,128)(2,1)S(1)} %all_to_all.11.x_ref), custom_call_target="tpu_custom_call" | custom-call | tf_op jit(solution)/shard_map/finish/pallas_call | solution.py:257
  (1 shorter events, 0.0 us)
Async XLA Ops:
  0.0 19.5 %collective-permute-start = (bf16[2,1024,1024]{2,1,0:T(8,128)(2,1)}, bf16[2,1024,1024]{2,1,0:T(8,128)(2,1)S(1)}, u32[]{:S(2)}, u32[]{:S(2)}) collective-permute-start(bf16[2,1024,1024]{2,1,0:T(8,128)(2,1)} %refs_0_.1), channel_id=1, source_target_pairs={{0,1},{1,0},{2,3},{3,2},{4,5},{5,4},{6,7},{7,6},{8,9},{9,8},{10,11... | collective-permute-start | bytes 12582920 | tf_op jit(solution)/shard_map/ppermute | solution.py:271
  0.5 19.1 %collective-permute-start.1 = (bf16[2,1024,1024]{2,1,0:T(8,128)(2,1)}, bf16[2,1024,1024]{2,1,0:T(8,128)(2,1)S(1)}, u32[]{:S(2)}, u32[]{:S(2)}) collective-permute-start(bf16[2,1024,1024]{2,1,0:T(8,128)(2,1)} %refs_1_.1), channel_id=1, source_target_pairs={{0,1},{1,0},{2,3},{3,2},{4,5},{5,4},{6,7},{7,6},{8,9},{9,8},{10,11... | collective-permute-start | bytes 12582920 | tf_op jit(solution)/shard_map/ppermute | solution.py:272
  1.3 18.3 %copy-start = (bf16[2,1024,1024]{2,1,0:T(8,128)(2,1)S(1)}, bf16[2,1024,1024]{2,1,0:T(8,128)(2,1)}, u32[]{:S(2)}) copy-start(bf16[2,1024,1024]{2,1,0:T(8,128)(2,1)} %refs_0_.1) | copy-start | bytes 12582916
  1.3 18.3 %copy-start.1 = (bf16[2,1024,1024]{2,1,0:T(8,128)(2,1)S(1)}, bf16[2,1024,1024]{2,1,0:T(8,128)(2,1)}, u32[]{:S(2)}) copy-start(bf16[2,1024,1024]{2,1,0:T(8,128)(2,1)} %refs_1_.1) | copy-start | bytes 12582916

commit v6 on v5

--- a/solution.py
+++ b/solution.py
@@ -110,10 +110,10 @@
     caches = [ref.at[:, :, mine] for ref in caches]
     ones = jnp.ones((KB, LANES), jnp.bfloat16)
     cap_lane = lane_iota((cap, LANES))
-    levels = []
-    for slot in range(local_shards):
-        level = jnp.zeros((cap, LANES), jnp.float32)
-        for g in range(kv_heads):
+    levels = [jnp.zeros((cap, LANES), jnp.float32) for _ in range(local_shards)]
+    for g in range(kv_heads):
+        for slot in range(local_shards):
+            level = levels[slot]
             columns = slice(g * HD, (g + 1) * HD)
             group_heads = [g * group + r for r in range(group)]
             query = jnp.concatenate(
@@ -142,13 +142,13 @@
             factors.append(jnp.zeros((SUBLANES - len(factors), packed), jnp.float32))
             factors = jnp.transpose(jnp.concatenate(factors, axis=0))
             total = sum(part * factors[:, i + 1:i + 2] for i, part in enumerate(sums))
-            average = total[:, :HD] / total[:, HD:]
+            average = total[:, :HD] * pl.reciprocal(total[:, HD:])
             log_total = factors[:, :1] + jnp.log2(total[:, HD:])
             for r, h in enumerate(group_heads):
                 at = slice(r * cap, (r + 1) * cap)
                 y_buf[slot, :, h * HD:(h + 1) * HD] = average[at]
                 level = jnp.where(cap_lane == h, log_total[at], level)
-        levels.append(level)
+            levels[slot] = level
 
     level_of = []
     for slot in range(local_shards):

time: 39.1 us -> 39 us (level)
  no operation moved by 1% of the time
where the time goes in v6:
time: 39 us; the launch traced here: 38.7 us
  blocking collectives  31.3 us (80%)
  Pallas kernels  6.12 us (16%)
  other arithmetic  0.75 us (2%)
  starting transfers between devices  0.51 us (1%)
    all_to_all x1, blocking collectives, shards(): received = lax.all_to_all(message, axes, 0, 0)  18.2 us
    all_to_all x1, blocking collectives, shards(): received = lax.all_to_all(partial, axes, 0, 0)  13.1 us
    pallas_call x1, Pallas kernels, attend(): pl.pallas_call(attend_body, out_shape=jax.ShapeDtypeStruct(message.shape,...  5.07 us
    pallas_call x1, Pallas kernels, finish(): pl.pallas_call(finish_body, out_shape=jax.ShapeDtypeStruct((own_rows, wid...  1.02 us
  transfers between devices with their start and end apart: 2, of which 0 were waited for; matrix products, arithmetic and copies ran while one was open for 2% of the time, Pallas kernels for 0%

profile of v6, /device:TPU:0, one launch (start us, length us, event | category | flops | bytes accessed | tf_op | source)
XLA Modules:
  0.0 38.7 jit_solution(8955159632871960037)
XLA Ops:
  0.0 0.5 %collective-permute-start = (bf16[2,1024,1024]{2,1,0:T(8,128)(2,1)}, bf16[2,1024,1024]{2,1,0:T(8,128)(2,1)S(1)}, u32[]{:S(2)}, u32[]{:S(2)}) collective-permute-start(bf16[2,1024,1024]{2,1,0:T(8,128)(2,1)} %refs_0_.1), channel_id=1, source_target_pairs={{0,1},{1,0},{2,3},{3,2},{4,5},{5,4},{6,7},{7,6},{8,9},{9,8},{10,11... | collective-permute-start | bytes 12582920 | tf_op jit(solution)/shard_map/ppermute | solution.py:271
  0.5 0.1 collective-permute-start.1
  0.5 0.8 %compare_select_fusion.x_ref = bf16[2,4224]{1,0:T(2,128)(2,1)S(1)} fusion(s32[2,8]{1,0:T(2,128)} %param.7, bf16[2,4096]{1,0:T(2,128)(2,1)} %param.4), kind=kLoop, calls=%fused_computation | loop fusion | flops 16896 | bytes 33344 | tf_op jit(solution)/shard_map/jit(_where)/select_n | solution.py:58
  1.3 0.0 copy-start
  1.3 0.0 copy-start.1
  1.3 18.2 %all_to_all.10.x_ref = bf16[32,2,2176]{2,1,0:T(2,128)(2,1)S(1)} all-to-all(bf16[32,2,2176]{2,1,0:T(2,128)(2,1)S(1)} %bitcast.1), channel_id=1, replica_groups=mesh['shard'=4,'seq'=8] {'shard','seq'}, dimensions={0} | all-to-all | bytes 557056 | tf_op jit(solution)/shard_map/all_to_all | solution.py:275
  19.5 0.0 collective-permute-done.refs_2_
  19.5 0.0 collective-permute-done.1.refs_3_
  19.5 0.0 copy-done
  19.5 0.0 copy-done.1
  19.5 5.1 %attend.1 = bf16[32,2,2176]{2,1,0:T(2,128)(2,1)S(1)} custom-call(bf16[32,2,2176]{2,1,0:T(2,128)(2,1)S(1)} %all_to_all.10.x_ref, bf16[2,1024,1024]{2,1,0:T(8,128)(2,1)S(1)} %copy-done, bf16[2,1024,1024]{2,1,0:T(8,128)(2,1)S(1)} %copy-done.1, bf16[2,1024,1024]{2,1,0:T(8,128)(2,1)S(1)} %collective-permute-done.refs_2_, ...), custom_call_target="tpu_custom_call" | custom-call | flops 1073741824 | bytes 8388608 | tf_op jit(solution)/shard_map/attend/pallas_call | solution.py:199
  24.6 13.1 %all_to_all.11.x_ref = bf16[32,2,2176]{2,1,0:T(2,128)(2,1)S(1)} all-to-all(bf16[32,2,2176]{2,1,0:T(2,128)(2,1)S(1)} %attend.1), channel_id=1, replica_groups=mesh['shard'=4,'seq'=8] {'shard','seq'}, dimensions={0} | all-to-all | bytes 557056 | tf_op jit(solution)/shard_map/all_to_all | solution.py:277
  37.7 1.0 %finish.1 = bf16[2,4096]{1,0:T(2,128)(2,1)} custom-call(bf16[32,2,2176]{2,1,0:T(2,128)(2,1)S(1)} %all_to_all.11.x_ref), custom_call_target="tpu_custom_call" | custom-call | tf_op jit(solution)/shard_map/finish/pallas_call | solution.py:257
  (1 shorter events, 0.0 us)
Async XLA Ops:
  0.0 19.5 %collective-permute-start = (bf16[2,1024,1024]{2,1,0:T(8,128)(2,1)}, bf16[2,1024,1024]{2,1,0:T(8,128)(2,1)S(1)}, u32[]{:S(2)}, u32[]{:S(2)}) collective-permute-start(bf16[2,1024,1024]{2,1,0:T(8,128)(2,1)} %refs_0_.1), channel_id=1, source_target_pairs={{0,1},{1,0},{2,3},{3,2},{4,5},{5,4},{6,7},{7,6},{8,9},{9,8},{10,11... | collective-permute-start | bytes 12582920 | tf_op jit(solution)/shard_map/ppermute | solution.py:271
  0.5 19.1 %collective-permute-start.1 = (bf16[2,1024,1024]{2,1,0:T(8,128)(2,1)}, bf16[2,1024,1024]{2,1,0:T(8,128)(2,1)S(1)}, u32[]{:S(2)}, u32[]{:S(2)}) collective-permute-start(bf16[2,1024,1024]{2,1,0:T(8,128)(2,1)} %refs_1_.1), channel_id=1, source_target_pairs={{0,1},{1,0},{2,3},{3,2},{4,5},{5,4},{6,7},{7,6},{8,9},{9,8},{10,11... | collective-permute-start | bytes 12582920 | tf_op jit(solution)/shard_map/ppermute | solution.py:272
  1.3 18.3 %copy-start = (bf16[2,1024,1024]{2,1,0:T(8,128)(2,1)S(1)}, bf16[2,1024,1024]{2,1,0:T(8,128)(2,1)}, u32[]{:S(2)}) copy-start(bf16[2,1024,1024]{2,1,0:T(8,128)(2,1)} %refs_0_.1) | copy-start | bytes 12582916
  1.3 18.3 %copy-start.1 = (bf16[2,1024,1024]{2,1,0:T(8,128)(2,1)S(1)}, bf16[2,1024,1024]{2,1,0:T(8,128)(2,1)}, u32[]{:S(2)}) copy-start(bf16[2,1024,1024]{2,1,0:T(8,128)(2,1)} %refs_1_.1) | copy-start | bytes 12582916

commit v7 on v6

--- a/solution.py
+++ b/solution.py
@@ -85,10 +85,7 @@
     listed = x[:, width:].astype(jnp.float32)
     first = lax.axis_index("shard") * local_shards
     lane = lane_iota((rows, LANES))
-    slots = jnp.zeros((rows, LANES), jnp.float32)
-    for slot in range(local_shards):
-        hit = jnp.sum(jnp.where(lane == first + slot, listed, 0.0), axis=1, keepdims=True)
-        slots = jnp.where(lane == slot, hit, slots)
+    slots = pltpu.roll(listed, lax.rem(LANES - first, LANES), 1)
     hits = [slots[:, slot:slot + 1] > 0.0 for slot in range(local_shards)]
     row = lax.broadcasted_iota(jnp.int32, (rows, rows), 0)
     column = lax.broadcasted_iota(jnp.int32, (rows, rows), 1)
@@ -141,7 +138,12 @@
             factors = [top] + [jnp.exp2(peak - top) for peak in peaks]
             factors.append(jnp.zeros((SUBLANES - len(factors), packed), jnp.float32))
             factors = jnp.transpose(jnp.concatenate(factors, axis=0))
-            total = sum(part * factors[:, i + 1:i + 2] for i, part in enumerate(sums))
+            spread = [
+                jnp.broadcast_to(factors[:, i + 1:i + 2], (packed, HD)) for i in range(len(sums))
+            ]
+            total = sum(
+                part * jnp.concatenate([factor] * 2, axis=1) for part, factor in zip(sums, spread)
+            )
             average = total[:, :HD] * pl.reciprocal(total[:, HD:])
             log_total = factors[:, :1] + jnp.log2(total[:, HD:])
             for r, h in enumerate(group_heads):
@@ -228,12 +230,14 @@
 
     x = x_ref[...].reshape(rows, message)
     stats = x[:, width:].astype(jnp.float32)
+    top = over_chips(stats.reshape(rows // SUBLANES, SUBLANES, LANES), jnp.maximum)[None]
     level = stats
     for i in (1, 2):
         level = level + pltpu.roll(stats, LANES - PART * i, 1)
     level = level.reshape(rows // SUBLANES, SUBLANES, LANES)
-    factor = jnp.exp2(level - over_chips(level, jnp.maximum)[None])
-    share = factor / over_chips(factor, jnp.add)[None]
+    factor = jnp.where(lane_iota(level.shape) < heads, jnp.exp2(level - top), 0.0)
+    total = over_chips(factor, jnp.add)[None]
+    share = factor * pl.reciprocal(jnp.where(total > 0.0, total, 1.0))
     share = jnp.transpose(share.reshape(rows, LANES))[:heads]
     high, low = parts_of(share, 2)
     target = lax.broadcasted_iota(jnp.int32, (SUBLANES, rows), 0)

time: 39 us -> 38.9 us (level)
  no operation moved by 1% of the time
where the time goes in v7:
time: 38.9 us; the launch traced here: 38.6 us
  blocking collectives  31.2 us (80%)
  Pallas kernels  6 us (15%)
  other arithmetic  0.75 us (2%)
  starting transfers between devices  0.51 us (1%)
    all_to_all x1, blocking collectives, shards(): received = lax.all_to_all(message, axes, 0, 0)  18.2 us
    all_to_all x1, blocking collectives, shards(): received = lax.all_to_all(partial, axes, 0, 0)  13.1 us
    pallas_call x1, Pallas kernels, attend(): pl.pallas_call(attend_body, out_shape=jax.ShapeDtypeStruct(message.shape,...  4.98 us
    pallas_call x1, Pallas kernels, finish(): pl.pallas_call(finish_body, out_shape=jax.ShapeDtypeStruct((own_rows, wid...  1 us
  transfers between devices with their start and end apart: 2, of which 0 were waited for; matrix products, arithmetic and copies ran while one was open for 2% of the time, Pallas kernels for 0%

profile of v7, /device:TPU:0, one launch (start us, length us, event | category | flops | bytes accessed | tf_op | source)
XLA Modules:
  0.0 38.6 jit_solution(2325589279958760147)
XLA Ops:
  0.0 0.5 %collective-permute-start = (bf16[2,1024,1024]{2,1,0:T(8,128)(2,1)}, bf16[2,1024,1024]{2,1,0:T(8,128)(2,1)S(1)}, u32[]{:S(2)}, u32[]{:S(2)}) collective-permute-start(bf16[2,1024,1024]{2,1,0:T(8,128)(2,1)} %refs_0_.1), channel_id=1, source_target_pairs={{0,1},{1,0},{2,3},{3,2},{4,5},{5,4},{6,7},{7,6},{8,9},{9,8},{10,11... | collective-permute-start | bytes 12582920 | tf_op jit(solution)/shard_map/ppermute | solution.py:275
  0.5 0.1 collective-permute-start.1
  0.5 0.8 %compare_select_fusion.x_ref = bf16[2,4224]{1,0:T(2,128)(2,1)S(1)} fusion(s32[2,8]{1,0:T(2,128)} %param.7, bf16[2,4096]{1,0:T(2,128)(2,1)} %param.4), kind=kLoop, calls=%fused_computation | loop fusion | flops 16896 | bytes 33344 | tf_op jit(solution)/shard_map/jit(_where)/select_n | solution.py:58
  1.3 0.0 copy-start
  1.3 0.0 copy-start.1
  1.3 18.2 %all_to_all.10.x_ref = bf16[32,2,2176]{2,1,0:T(2,128)(2,1)S(1)} all-to-all(bf16[32,2,2176]{2,1,0:T(2,128)(2,1)S(1)} %bitcast.1), channel_id=1, replica_groups=mesh['shard'=4,'seq'=8] {'shard','seq'}, dimensions={0} | all-to-all | bytes 557056 | tf_op jit(solution)/shard_map/all_to_all | solution.py:279
  19.5 0.0 collective-permute-done.refs_2_
  19.5 0.0 collective-permute-done.1.refs_3_
  19.5 0.0 copy-done
  19.5 0.0 copy-done.1
  19.5 5.0 %attend.1 = bf16[32,2,2176]{2,1,0:T(2,128)(2,1)S(1)} custom-call(bf16[32,2,2176]{2,1,0:T(2,128)(2,1)S(1)} %all_to_all.10.x_ref, bf16[2,1024,1024]{2,1,0:T(8,128)(2,1)S(1)} %copy-done, bf16[2,1024,1024]{2,1,0:T(8,128)(2,1)S(1)} %copy-done.1, bf16[2,1024,1024]{2,1,0:T(8,128)(2,1)S(1)} %collective-permute-done.refs_2_, ...), custom_call_target="tpu_custom_call" | custom-call | flops 1073741824 | bytes 8388608 | tf_op jit(solution)/shard_map/attend/pallas_call | solution.py:201
  24.5 13.1 %all_to_all.11.x_ref = bf16[32,2,2176]{2,1,0:T(2,128)(2,1)S(1)} all-to-all(bf16[32,2,2176]{2,1,0:T(2,128)(2,1)S(1)} %attend.1), channel_id=1, replica_groups=mesh['shard'=4,'seq'=8] {'shard','seq'}, dimensions={0} | all-to-all | bytes 557056 | tf_op jit(solution)/shard_map/all_to_all | solution.py:281
  37.6 1.0 %finish.1 = bf16[2,4096]{1,0:T(2,128)(2,1)} custom-call(bf16[32,2,2176]{2,1,0:T(2,128)(2,1)S(1)} %all_to_all.11.x_ref), custom_call_target="tpu_custom_call" | custom-call | tf_op jit(solution)/shard_map/finish/pallas_call | solution.py:261
  (1 shorter events, 0.0 us)
Async XLA Ops:
  0.0 19.5 %collective-permute-start = (bf16[2,1024,1024]{2,1,0:T(8,128)(2,1)}, bf16[2,1024,1024]{2,1,0:T(8,128)(2,1)S(1)}, u32[]{:S(2)}, u32[]{:S(2)}) collective-permute-start(bf16[2,1024,1024]{2,1,0:T(8,128)(2,1)} %refs_0_.1), channel_id=1, source_target_pairs={{0,1},{1,0},{2,3},{3,2},{4,5},{5,4},{6,7},{7,6},{8,9},{9,8},{10,11... | collective-permute-start | bytes 12582920 | tf_op jit(solution)/shard_map/ppermute | solution.py:275
  0.5 19.1 %collective-permute-start.1 = (bf16[2,1024,1024]{2,1,0:T(8,128)(2,1)}, bf16[2,1024,1024]{2,1,0:T(8,128)(2,1)S(1)}, u32[]{:S(2)}, u32[]{:S(2)}) collective-permute-start(bf16[2,1024,1024]{2,1,0:T(8,128)(2,1)} %refs_1_.1), channel_id=1, source_target_pairs={{0,1},{1,0},{2,3},{3,2},{4,5},{5,4},{6,7},{7,6},{8,9},{9,8},{10,11... | collective-permute-start | bytes 12582920 | tf_op jit(solution)/shard_map/ppermute | solution.py:276
  1.3 18.3 %copy-start = (bf16[2,1024,1024]{2,1,0:T(8,128)(2,1)S(1)}, bf16[2,1024,1024]{2,1,0:T(8,128)(2,1)}, u32[]{:S(2)}) copy-start(bf16[2,1024,1024]{2,1,0:T(8,128)(2,1)} %refs_0_.1) | copy-start | bytes 12582916
  1.3 18.3 %copy-start.1 = (bf16[2,1024,1024]{2,1,0:T(8,128)(2,1)S(1)}, bf16[2,1024,1024]{2,1,0:T(8,128)(2,1)}, u32[]{:S(2)}) copy-start(bf16[2,1024,1024]{2,1,0:T(8,128)(2,1)} %refs_1_.1) | copy-start | bytes 12582916

commit v8 on v7

--- a/solution.py
+++ b/solution.py
@@ -99,12 +99,14 @@
         picks.append(
             one_hot((pick_at == place_t[slot:slot + 1]) & (slots_t[slot:slot + 1] > 0.0))
         )
-        q_buf[slot] = dot(picks[slot], x[:, :width]).astype(jnp.bfloat16)
         back_at = lax.rem(lane_iota((rows, 3 * cap)), cap).astype(jnp.float32)
         backs.append(one_hot((back_at == place[:, slot:slot + 1]) & hits[slot]))
 
     mine = pl.ds(pl.multiple_of(first_column, HD), kv_heads * HD)
     caches = [ref.at[:, :, mine] for ref in caches]
+    picked = dot(jnp.concatenate(picks, axis=0), x[:, :width]).astype(jnp.bfloat16)
+    for slot in range(local_shards):
+        q_buf[slot] = picked[slot * cap:(slot + 1) * cap]
     ones = jnp.ones((KB, LANES), jnp.bfloat16)
     cap_lane = lane_iota((cap, LANES))
     levels = [jnp.zeros((cap, LANES), jnp.float32) for _ in range(local_shards)]

time: 38.9 us -> 38.8 us (level)
  no operation moved by 1% of the time
where the time goes in v8:
time: 38.8 us; the launch traced here: 38.6 us
  blocking collectives  31.3 us (81%)
  Pallas kernels  5.99 us (15%)
  other arithmetic  0.75 us (2%)
  starting transfers between devices  0.51 us (1%)
    all_to_all x1, blocking collectives, shards(): received = lax.all_to_all(message, axes, 0, 0)  18.2 us
    all_to_all x1, blocking collectives, shards(): received = lax.all_to_all(partial, axes, 0, 0)  13.1 us
    pallas_call x1, Pallas kernels, attend(): pl.pallas_call(attend_body, out_shape=jax.ShapeDtypeStruct(message.shape,...  4.96 us
    pallas_call x1, Pallas kernels, finish(): pl.pallas_call(finish_body, out_shape=jax.ShapeDtypeStruct((own_rows, wid...  1 us
  transfers between devices with their start and end apart: 2, of which 0 were waited for; matrix products, arithmetic and copies ran while one was open for 2% of the time, Pallas kernels for 0%

profile of v8, /device:TPU:0, one launch (start us, length us, event | category | flops | bytes accessed | tf_op | source)
XLA Modules:
  0.0 38.6 jit_solution(16635735835794547895)
XLA Ops:
  0.0 0.5 %collective-permute-start = (bf16[2,1024,1024]{2,1,0:T(8,128)(2,1)}, bf16[2,1024,1024]{2,1,0:T(8,128)(2,1)S(1)}, u32[]{:S(2)}, u32[]{:S(2)}) collective-permute-start(bf16[2,1024,1024]{2,1,0:T(8,128)(2,1)} %refs_0_.1), channel_id=1, source_target_pairs={{0,1},{1,0},{2,3},{3,2},{4,5},{5,4},{6,7},{7,6},{8,9},{9,8},{10,11... | collective-permute-start | bytes 12582920 | tf_op jit(solution)/shard_map/ppermute | solution.py:277
  0.5 0.1 collective-permute-start.1
  0.5 0.8 %compare_select_fusion.x_ref = bf16[2,4224]{1,0:T(2,128)(2,1)S(1)} fusion(s32[2,8]{1,0:T(2,128)} %param.7, bf16[2,4096]{1,0:T(2,128)(2,1)} %param.4), kind=kLoop, calls=%fused_computation | loop fusion | flops 16896 | bytes 33344 | tf_op jit(solution)/shard_map/jit(_where)/select_n | solution.py:58
  1.3 0.0 copy-start
  1.3 0.0 copy-start.1
  1.3 18.2 %all_to_all.10.x_ref = bf16[32,2,2176]{2,1,0:T(2,128)(2,1)S(1)} all-to-all(bf16[32,2,2176]{2,1,0:T(2,128)(2,1)S(1)} %bitcast.1), channel_id=1, replica_groups=mesh['shard'=4,'seq'=8] {'shard','seq'}, dimensions={0} | all-to-all | bytes 557056 | tf_op jit(solution)/shard_map/all_to_all | solution.py:281
  19.5 0.0 collective-permute-done.refs_2_
  19.5 0.0 collective-permute-done.1.refs_3_
  19.5 0.0 copy-done
  19.5 0.0 copy-done.1
  19.5 5.0 %attend.1 = bf16[32,2,2176]{2,1,0:T(2,128)(2,1)S(1)} custom-call(bf16[32,2,2176]{2,1,0:T(2,128)(2,1)S(1)} %all_to_all.10.x_ref, bf16[2,1024,1024]{2,1,0:T(8,128)(2,1)S(1)} %copy-done, bf16[2,1024,1024]{2,1,0:T(8,128)(2,1)S(1)} %copy-done.1, bf16[2,1024,1024]{2,1,0:T(8,128)(2,1)S(1)} %collective-permute-done.refs_2_, ...), custom_call_target="tpu_custom_call" | custom-call | flops 1073741824 | bytes 8388608 | tf_op jit(solution)/shard_map/attend/pallas_call | solution.py:203
  24.5 13.1 %all_to_all.11.x_ref = bf16[32,2,2176]{2,1,0:T(2,128)(2,1)S(1)} all-to-all(bf16[32,2,2176]{2,1,0:T(2,128)(2,1)S(1)} %attend.1), channel_id=1, replica_groups=mesh['shard'=4,'seq'=8] {'shard','seq'}, dimensions={0} | all-to-all | bytes 557056 | tf_op jit(solution)/shard_map/all_to_all | solution.py:283
  37.6 1.0 %finish.1 = bf16[2,4096]{1,0:T(2,128)(2,1)} custom-call(bf16[32,2,2176]{2,1,0:T(2,128)(2,1)S(1)} %all_to_all.11.x_ref), custom_call_target="tpu_custom_call" | custom-call | tf_op jit(solution)/shard_map/finish/pallas_call | solution.py:263
  (1 shorter events, 0.0 us)
Async XLA Ops:
  0.0 19.5 %collective-permute-start = (bf16[2,1024,1024]{2,1,0:T(8,128)(2,1)}, bf16[2,1024,1024]{2,1,0:T(8,128)(2,1)S(1)}, u32[]{:S(2)}, u32[]{:S(2)}) collective-permute-start(bf16[2,1024,1024]{2,1,0:T(8,128)(2,1)} %refs_0_.1), channel_id=1, source_target_pairs={{0,1},{1,0},{2,3},{3,2},{4,5},{5,4},{6,7},{7,6},{8,9},{9,8},{10,11... | collective-permute-start | bytes 12582920 | tf_op jit(solution)/shard_map/ppermute | solution.py:277
  0.5 19.1 %collective-permute-start.1 = (bf16[2,1024,1024]{2,1,0:T(8,128)(2,1)}, bf16[2,1024,1024]{2,1,0:T(8,128)(2,1)S(1)}, u32[]{:S(2)}, u32[]{:S(2)}) collective-permute-start(bf16[2,1024,1024]{2,1,0:T(8,128)(2,1)} %refs_1_.1), channel_id=1, source_target_pairs={{0,1},{1,0},{2,3},{3,2},{4,5},{5,4},{6,7},{7,6},{8,9},{9,8},{10,11... | collective-permute-start | bytes 12582920 | tf_op jit(solution)/shard_map/ppermute | solution.py:278
  1.3 18.3 %copy-start = (bf16[2,1024,1024]{2,1,0:T(8,128)(2,1)S(1)}, bf16[2,1024,1024]{2,1,0:T(8,128)(2,1)}, u32[]{:S(2)}) copy-start(bf16[2,1024,1024]{2,1,0:T(8,128)(2,1)} %refs_0_.1) | copy-start | bytes 12582916
  1.3 18.3 %copy-start.1 = (bf16[2,1024,1024]{2,1,0:T(8,128)(2,1)S(1)}, bf16[2,1024,1024]{2,1,0:T(8,128)(2,1)}, u32[]{:S(2)}) copy-start(bf16[2,1024,1024]{2,1,0:T(8,128)(2,1)} %refs_1_.1) | copy-start | bytes 12582916

commit v9 on v8

--- a/solution.py
+++ b/solution.py
@@ -247,12 +247,19 @@
     mine = target == lax.rem(source, period)
     high, low = high.astype(jnp.float32), low.astype(jnp.float32)
     pieces = []
-    for h in range(heads):
+    for pair in range(0, heads, 2):
         weights = jnp.concatenate(
-            [jnp.where(mine, part[h:h + 1], 0.0) for part in (high, low)], axis=0
+            [
+                jnp.where(mine, part[h:h + 1], 0.0)
+                for h in (pair, pair + 1)
+                for part in (high, low)
+            ],
+            axis=0,
         ).astype(jnp.bfloat16)
-        both = dot(weights, x[:, h * HD:(h + 1) * HD])
-        pieces.append(both[:SUBLANES] + both[SUBLANES:])
+        both = dot(weights, x[:, pair * HD:(pair + 2) * HD])
+        for i in range(2):
+            part = both[2 * i * SUBLANES:2 * (i + 1) * SUBLANES, i * HD:(i + 1) * HD]
+            pieces.append(part[:SUBLANES] + part[SUBLANES:])
     merged = jnp.concatenate(pieces, axis=1)
     out_ref[...] = jnp.concatenate(
         [merged[core * own_rows:(core + 1) * own_rows] for core in range(2)], axis=1

time: 38.8 us -> 38.8 us (level)
  no operation moved by 1% of the time
where the time goes in v9:
time: 38.8 us; the launch traced here: 38.5 us
  blocking collectives  31.3 us (81%)
  Pallas kernels  5.96 us (15%)
  other arithmetic  0.75 us (2%)
  starting transfers between devices  0.51 us (1%)
    all_to_all x1, blocking collectives, shards(): received = lax.all_to_all(message, axes, 0, 0)  18.2 us
    all_to_all x1, blocking collectives, shards(): received = lax.all_to_all(partial, axes, 0, 0)  13.1 us
    pallas_call x1, Pallas kernels, attend(): pl.pallas_call(attend_body, out_shape=jax.ShapeDtypeStruct(message.shape,...  4.96 us
    pallas_call x1, Pallas kernels, finish(): pl.pallas_call(finish_body, out_shape=jax.ShapeDtypeStruct((own_rows, wid...  0.97 us
  transfers between devices with their start and end apart: 2, of which 0 were waited for; matrix products, arithmetic and copies ran while one was open for 2% of the time, Pallas kernels for 0%

profile of v9, /device:TPU:0, one launch (start us, length us, event | category | flops | bytes accessed | tf_op | source)
XLA Modules:
  0.0 38.5 jit_solution(3386511199680543454)
XLA Ops:
  0.0 0.5 %collective-permute-start = (bf16[2,1024,1024]{2,1,0:T(8,128)(2,1)}, bf16[2,1024,1024]{2,1,0:T(8,128)(2,1)S(1)}, u32[]{:S(2)}, u32[]{:S(2)}) collective-permute-start(bf16[2,1024,1024]{2,1,0:T(8,128)(2,1)} %refs_0_.1), channel_id=1, source_target_pairs={{0,1},{1,0},{2,3},{3,2},{4,5},{5,4},{6,7},{7,6},{8,9},{9,8},{10,11... | collective-permute-start | bytes 12582920 | tf_op jit(solution)/shard_map/ppermute | solution.py:284
  0.5 0.1 collective-permute-start.1
  0.5 0.8 %compare_select_fusion.x_ref = bf16[2,4224]{1,0:T(2,128)(2,1)S(1)} fusion(s32[2,8]{1,0:T(2,128)} %param.7, bf16[2,4096]{1,0:T(2,128)(2,1)} %param.4), kind=kLoop, calls=%fused_computation | loop fusion | flops 16896 | bytes 33344 | tf_op jit(solution)/shard_map/jit(_where)/select_n | solution.py:58
  1.3 0.0 copy-start
  1.3 0.0 copy-start.1
  1.3 18.2 %all_to_all.10.x_ref = bf16[32,2,2176]{2,1,0:T(2,128)(2,1)S(1)} all-to-all(bf16[32,2,2176]{2,1,0:T(2,128)(2,1)S(1)} %bitcast.1), channel_id=1, replica_groups=mesh['shard'=4,'seq'=8] {'shard','seq'}, dimensions={0} | all-to-all | bytes 557056 | tf_op jit(solution)/shard_map/all_to_all | solution.py:288
  19.5 0.0 collective-permute-done.refs_2_
  19.5 0.0 collective-permute-done.1.refs_3_
  19.5 0.0 copy-done
  19.5 0.0 copy-done.1
  19.5 5.0 %attend.1 = bf16[32,2,2176]{2,1,0:T(2,128)(2,1)S(1)} custom-call(bf16[32,2,2176]{2,1,0:T(2,128)(2,1)S(1)} %all_to_all.10.x_ref, bf16[2,1024,1024]{2,1,0:T(8,128)(2,1)S(1)} %copy-done, bf16[2,1024,1024]{2,1,0:T(8,128)(2,1)S(1)} %copy-done.1, bf16[2,1024,1024]{2,1,0:T(8,128)(2,1)S(1)} %collective-permute-done.refs_2_, ...), custom_call_target="tpu_custom_call" | custom-call | flops 1073741824 | bytes 8388608 | tf_op jit(solution)/shard_map/attend/pallas_call | solution.py:203
  24.5 13.1 %all_to_all.11.x_ref = bf16[32,2,2176]{2,1,0:T(2,128)(2,1)S(1)} all-to-all(bf16[32,2,2176]{2,1,0:T(2,128)(2,1)S(1)} %attend.1), channel_id=1, replica_groups=mesh['shard'=4,'seq'=8] {'shard','seq'}, dimensions={0} | all-to-all | bytes 557056 | tf_op jit(solution)/shard_map/all_to_all | solution.py:290
  37.6 1.0 %finish.1 = bf16[2,4096]{1,0:T(2,128)(2,1)} custom-call(bf16[32,2,2176]{2,1,0:T(2,128)(2,1)S(1)} %all_to_all.11.x_ref), custom_call_target="tpu_custom_call" | custom-call | tf_op jit(solution)/shard_map/finish/pallas_call | solution.py:270
  (1 shorter events, 0.0 us)
Async XLA Ops:
  0.0 19.5 %collective-permute-start = (bf16[2,1024,1024]{2,1,0:T(8,128)(2,1)}, bf16[2,1024,1024]{2,1,0:T(8,128)(2,1)S(1)}, u32[]{:S(2)}, u32[]{:S(2)}) collective-permute-start(bf16[2,1024,1024]{2,1,0:T(8,128)(2,1)} %refs_0_.1), channel_id=1, source_target_pairs={{0,1},{1,0},{2,3},{3,2},{4,5},{5,4},{6,7},{7,6},{8,9},{9,8},{10,11... | collective-permute-start | bytes 12582920 | tf_op jit(solution)/shard_map/ppermute | solution.py:284
  0.5 19.1 %collective-permute-start.1 = (bf16[2,1024,1024]{2,1,0:T(8,128)(2,1)}, bf16[2,1024,1024]{2,1,0:T(8,128)(2,1)S(1)}, u32[]{:S(2)}, u32[]{:S(2)}) collective-permute-start(bf16[2,1024,1024]{2,1,0:T(8,128)(2,1)} %refs_1_.1), channel_id=1, source_target_pairs={{0,1},{1,0},{2,3},{3,2},{4,5},{5,4},{6,7},{7,6},{8,9},{9,8},{10,11... | collective-permute-start | bytes 12582920 | tf_op jit(solution)/shard_map/ppermute | solution.py:285
  1.3 18.3 %copy-start = (bf16[2,1024,1024]{2,1,0:T(8,128)(2,1)S(1)}, bf16[2,1024,1024]{2,1,0:T(8,128)(2,1)}, u32[]{:S(2)}) copy-start(bf16[2,1024,1024]{2,1,0:T(8,128)(2,1)} %refs_0_.1) | copy-start | bytes 12582916
  1.3 18.3 %copy-start.1 = (bf16[2,1024,1024]{2,1,0:T(8,128)(2,1)S(1)}, bf16[2,1024,1024]{2,1,0:T(8,128)(2,1)}, u32[]{:S(2)}) copy-start(bf16[2,1024,1024]{2,1,0:T(8,128)(2,1)} %refs_1_.1) | copy-start | bytes 12582916
